TPU v7x, 32 devices: a whole 2x2x4 slice. The times are simulated.
32 devices in a mesh: row: 8 (over y, x, core), col: 4 (over z).
Axes of the slice: x: 2, y: 2, z: 4, core: 2. Of those that a mesh axis runs over, the one named last changes fastest.
Arguments:
- a_blocks: float32 [8, 8, 12, 128, 128], P('row', 'col'), may hold values from -0.5 to 0.5
- b_blocks: float32 [8, 4, 20, 128, 128], P('row', 'col'), may hold values from -5 to 5
- product_lists: int32 [8, 4, 8, 64, 3], P('row', 'col'), may hold values from 0 to 48, as said below
Outputs:
- c_blocks: float32 [8, 4, 48, 128, 128], P('row', 'col')
Inputs may be any that keep to these rules, and one draw needn't show every extreme that they name: `product_lists`: entry 0 of a product is a slot of the A panel, entry 1 a slot of the B panel, entry 2 a slot of the C panel or 48 for padding. In every list the real products come first, at least 21 of them; some lists of every draw have no padding.
All inputs are finite; a program needn't handle non-finite values.
Results may differ from a plain program's by a relative error of at most 0.0003.
Values sent between devices are 32-bit elements; how exact they have to be, the bound alone decides.
No kernel may reach another device: no remote copies, remote signals or barrier semaphores. Data moves between devices by JAX's collectives and lax.ppermute only.
A program may use at most 128 MiB of HBM per device.

v0:
```python
import jax
import jax.numpy as jnp
from jax import lax
from jax.sharding import PartitionSpec as P

SC = 48


def spread(block, axis, source):
    block = jnp.where(lax.axis_index(axis) == source, block, jnp.zeros_like(block))
    return lax.psum(block, axis)


def from_behind(value, axis, steps):
    count = lax.axis_size(axis)
    pairs = [(source, (source + steps) % count) for source in range(count)]
    return lax.ppermute(value, axis, pairs)


def apply_panel(totals, left, right, entries):
    left_sel = jnp.take(left, entries[:, 0], axis=0)
    right_sel = jnp.take(right, entries[:, 1], axis=0)
    terms = jnp.einsum("pij,pjk->pik", left_sel, right_sel, precision=lax.Precision.HIGHEST)
    count = entries.shape[0]
    onehot = (entries[:, 2][None, :] == jnp.arange(SC, dtype=jnp.int32)[:, None]).astype(
        jnp.float32
    )
    summed = jnp.dot(onehot, terms.reshape(count, -1), precision=lax.Precision.HIGHEST)
    return totals + summed.reshape(totals.shape)


def on_device(a_blocks, b_blocks, product_lists):
    rows = lax.axis_size("row")
    row_index = lax.axis_index("row")
    left_local = a_blocks[0]
    right_local = b_blocks[0, 0]
    lists_local = product_lists[0, 0]
    per_device = left_local.shape[0]

    def left_for(panel):
        mine = lax.dynamic_index_in_dim(left_local, panel % per_device, 0, keepdims=False)
        return spread(mine, "col", panel // per_device)

    def entries_for(panel):
        return lax.dynamic_index_in_dim(lists_local, panel, 0, keepdims=False)

    def do_panel(totals, panel, right):
        return apply_panel(totals, left_for(panel), right, entries_for(panel))

    start = jnp.zeros((SC, right_local.shape[1], right_local.shape[2]), jnp.float32)
    totals = do_panel(start, row_index, right_local)

    def turn_one(step, carry):
        acc, current = carry
        current = from_behind(current, "row", 1)
        acc = do_panel(acc, (row_index - step) % rows, current)
        return (acc, current)

    totals, current = lax.fori_loop(1, rows, turn_one, (totals, right_local))
    return totals.reshape(1, 1, totals.shape[0], totals.shape[1], totals.shape[2])


def solution(mesh):
    return jax.shard_map(
        on_device,
        mesh=mesh,
        in_specs=(
            P("row", "col", None, None, None),
            P("row", "col", None, None, None),
            P("row", "col", None, None, None),
        ),
        out_specs=P("row", "col", None, None, None),
        check_vma=False,
    )
```

profile of v0, /device:TPU:0, one launch (start us, length us, event | category | flops | bytes accessed | tf_op | source)
XLA Modules:
  0.0 558.3 jit_solution(15373643108157424537)
XLA Ops:
  10.1 2.8 gather_fusion.3
  12.8 43.7 %all-reduce.3.cloned.1.call-done = f32[12,128,128]{2,1,0:T(8,128)} async-done(((f32[12,128,128]{2,1,0:T(8,128)}), f32[12,128,128]{2,1,0:T(8,128)}) %all-reduce.3.cloned.1.call-update) | async-done | bytes 786448 | tf_op jit(solution)/shard_map/psum | solution.py:11
  56.5 3.9 gather_fusion.2
  60.4 7.1 %fusion.19 = f32[64,128,128]{2,1,0:T(8,128)S(1)} fusion(f32[64,128,128]{2,1,0:T(8,128)} %gather_fusion.3, f32[64,128,128]{2,1,0:T(8,128)} %gather_fusion.2, pred[64]{0:T(512)(128)(4,1)S(1)} %get-tuple-element.216, pred[64]{0:T(512)(128)(4,1)S(1)} %get-tuple-element.208), kind=kOutput, calls=%fused_computation.32 | convolution fusion | flops 1612709888 | bytes 12583040 | tf_op jit(solution)/shard_map/pij,pjk->pik/dot_general | solution.py:23
  67.5 6.2 %fusion.16 = f32[48,128,128]{2,0,1:T(8,128)} fusion(s32[64]{0:T(128)S(1)} %slice_bitcast_fusion.1, f32[8,8,128,128]{3,2,1,0:T(8,128)S(1)} %bitcast.86), kind=kOutput, calls=%fused_computation.29 | convolution fusion | flops 603982848 | bytes 7340288 | tf_op jit(solution)/shard_map/dot_general | solution.py:28
  73.7 473.2 %while.18 = (s32[]{:T(128)}, f32[48,128,128]{2,0,1:T(8,128)}, f32[20,128,128]{2,1,0:T(8,128)S(1)}, s32[]{:T(128)}, s32[8,64,3]{1,2,0:T(4,128)S(1)}, /*index=5*/f...) while((s32[]{:T(128)}, f32[48,128,128]{2,0,1:T(8,128)}, ...), condition=%wide.region_3.6_spmd, body=%wide.region_1.5_spmd.sunk | while | flops 2217875200 | bytes 79180944 | solution.py:59
  73.7 2.1 select_bitcast_fusion.3
  75.9 44.1 %all-reduce.5.cloned.1.call-done = f32[12,128,128]{2,1,0:T(8,128)} async-done(((f32[12,128,128]{2,1,0:T(8,128)}), f32[12,128,128]{2,1,0:T(8,128)}) %all-reduce.5.cloned.1.call-update) | async-done | bytes 786448 | tf_op jit(solution)/shard_map/while/body/eval_jaxpr/psum | solution.py:11
  119.9 3.9 gather_fusion.1
  123.8 2.8 gather_fusion
  126.6 7.2 %fusion.39 = f32[64,128,128]{2,1,0:T(8,128)S(1)} fusion(f32[64,128,128]{2,1,0:T(8,128)} %gather_fusion, f32[64,128,128]{2,1,0:T(8,128)} %gather_fusion.1, pred[64]{0:T(512)(128)(4,1)S(1)} %get-tuple-element.267, pred[64]{0:T(512)(128)(4,1)S(1)} %get-tuple-element.268), kind=kOutput, calls=%fused_computation.8.clone.1 | convolution fusion | flops 1612709888 | bytes 12583040 | tf_op jit(solution)/shard_map/while/body/eval_jaxpr/pij,pjk->pik/dot_general | solution.py:23
  133.9 5.8 %fusion.40 = f32[48,128,128]{2,0,1:T(8,128)S(1)} fusion(f32[48,128,128]{2,0,1:T(8,128)S(1)} %copy-done, s32[64]{0:T(128)S(1)} %slice_bitcast_fusion.3, f32[8,8,128,128]{3,2,1,0:T(8,128)S(1)} %bitcast.83), kind=kOutput, calls=%fused_computation.14.clone.1 | convolution fusion | flops 604769280 | bytes 10486016 | tf_op jit(solution)/shard_map/while/body/eval_jaxpr/dot_general | solution.py:28
  141.4 2.1 select_bitcast_fusion.3
  143.6 44.0 %all-reduce.5.cloned.1.call-done = f32[12,128,128]{2,1,0:T(8,128)} async-done(((f32[12,128,128]{2,1,0:T(8,128)}), f32[12,128,128]{2,1,0:T(8,128)}) %all-reduce.5.cloned.1.call-update) | async-done | bytes 786448 | tf_op jit(solution)/shard_map/while/body/eval_jaxpr/psum | solution.py:11
  187.7 3.9 gather_fusion.1
  191.6 2.8 gather_fusion
  194.4 7.2 %fusion.39 = f32[64,128,128]{2,1,0:T(8,128)S(1)} fusion(f32[64,128,128]{2,1,0:T(8,128)} %gather_fusion, f32[64,128,128]{2,1,0:T(8,128)} %gather_fusion.1, pred[64]{0:T(512)(128)(4,1)S(1)} %get-tuple-element.267, pred[64]{0:T(512)(128)(4,1)S(1)} %get-tuple-element.268), kind=kOutput, calls=%fused_computation.8.clone.1 | convolution fusion | flops 1612709888 | bytes 12583040 | tf_op jit(solution)/shard_map/while/body/eval_jaxpr/pij,pjk->pik/dot_general | solution.py:23
  201.6 5.8 %fusion.40 = f32[48,128,128]{2,0,1:T(8,128)S(1)} fusion(f32[48,128,128]{2,0,1:T(8,128)S(1)} %copy-done, s32[64]{0:T(128)S(1)} %slice_bitcast_fusion.3, f32[8,8,128,128]{3,2,1,0:T(8,128)S(1)} %bitcast.83), kind=kOutput, calls=%fused_computation.14.clone.1 | convolution fusion | flops 604769280 | bytes 10486016 | tf_op jit(solution)/shard_map/while/body/eval_jaxpr/dot_general | solution.py:28
  209.2 2.1 select_bitcast_fusion.3
  211.3 43.7 %all-reduce.5.cloned.1.call-done = f32[12,128,128]{2,1,0:T(8,128)} async-done(((f32[12,128,128]{2,1,0:T(8,128)}), f32[12,128,128]{2,1,0:T(8,128)}) %all-reduce.5.cloned.1.call-update) | async-done | bytes 786448 | tf_op jit(solution)/shard_map/while/body/eval_jaxpr/psum | solution.py:11
  255.1 3.9 gather_fusion.1
  259.0 2.8 gather_fusion
  261.8 7.2 %fusion.39 = f32[64,128,128]{2,1,0:T(8,128)S(1)} fusion(f32[64,128,128]{2,1,0:T(8,128)} %gather_fusion, f32[64,128,128]{2,1,0:T(8,128)} %gather_fusion.1, pred[64]{0:T(512)(128)(4,1)S(1)} %get-tuple-element.267, pred[64]{0:T(512)(128)(4,1)S(1)} %get-tuple-element.268), kind=kOutput, calls=%fused_computation.8.clone.1 | convolution fusion | flops 1612709888 | bytes 12583040 | tf_op jit(solution)/shard_map/while/body/eval_jaxpr/pij,pjk->pik/dot_general | solution.py:23
  269.0 5.8 %fusion.40 = f32[48,128,128]{2,0,1:T(8,128)S(1)} fusion(f32[48,128,128]{2,0,1:T(8,128)S(1)} %copy-done, s32[64]{0:T(128)S(1)} %slice_bitcast_fusion.3, f32[8,8,128,128]{3,2,1,0:T(8,128)S(1)} %bitcast.83), kind=kOutput, calls=%fused_computation.14.clone.1 | convolution fusion | flops 604769280 | bytes 10486016 | tf_op jit(solution)/shard_map/while/body/eval_jaxpr/dot_general | solution.py:28
  276.6 2.1 select_bitcast_fusion.3
  278.8 43.7 %all-reduce.5.cloned.1.call-done = f32[12,128,128]{2,1,0:T(8,128)} async-done(((f32[12,128,128]{2,1,0:T(8,128)}), f32[12,128,128]{2,1,0:T(8,128)}) %all-reduce.5.cloned.1.call-update) | async-done | bytes 786448 | tf_op jit(solution)/shard_map/while/body/eval_jaxpr/psum | solution.py:11
  322.5 3.9 gather_fusion.1
  326.4 2.8 gather_fusion
  329.2 7.2 %fusion.39 = f32[64,128,128]{2,1,0:T(8,128)S(1)} fusion(f32[64,128,128]{2,1,0:T(8,128)} %gather_fusion, f32[64,128,128]{2,1,0:T(8,128)} %gather_fusion.1, pred[64]{0:T(512)(128)(4,1)S(1)} %get-tuple-element.267, pred[64]{0:T(512)(128)(4,1)S(1)} %get-tuple-element.268), kind=kOutput, calls=%fused_computation.8.clone.1 | convolution fusion | flops 1612709888 | bytes 12583040 | tf_op jit(solution)/shard_map/while/body/eval_jaxpr/pij,pjk->pik/dot_general | solution.py:23
  336.4 5.8 %fusion.40 = f32[48,128,128]{2,0,1:T(8,128)S(1)} fusion(f32[48,128,128]{2,0,1:T(8,128)S(1)} %copy-done, s32[64]{0:T(128)S(1)} %slice_bitcast_fusion.3, f32[8,8,128,128]{3,2,1,0:T(8,128)S(1)} %bitcast.83), kind=kOutput, calls=%fused_computation.14.clone.1 | convolution fusion | flops 604769280 | bytes 10486016 | tf_op jit(solution)/shard_map/while/body/eval_jaxpr/dot_general | solution.py:28
  344.0 2.1 select_bitcast_fusion.3
  346.2 43.7 %all-reduce.5.cloned.1.call-done = f32[12,128,128]{2,1,0:T(8,128)} async-done(((f32[12,128,128]{2,1,0:T(8,128)}), f32[12,128,128]{2,1,0:T(8,128)}) %all-reduce.5.cloned.1.call-update) | async-done | bytes 786448 | tf_op jit(solution)/shard_map/while/body/eval_jaxpr/psum | solution.py:11
  389.9 3.9 gather_fusion.1
  393.8 2.8 gather_fusion
  396.6 7.2 %fusion.39 = f32[64,128,128]{2,1,0:T(8,128)S(1)} fusion(f32[64,128,128]{2,1,0:T(8,128)} %gather_fusion, f32[64,128,128]{2,1,0:T(8,128)} %gather_fusion.1, pred[64]{0:T(512)(128)(4,1)S(1)} %get-tuple-element.267, pred[64]{0:T(512)(128)(4,1)S(1)} %get-tuple-element.268), kind=kOutput, calls=%fused_computation.8.clone.1 | convolution fusion | flops 1612709888 | bytes 12583040 | tf_op jit(solution)/shard_map/while/body/eval_jaxpr/pij,pjk->pik/dot_general | solution.py:23
  403.9 5.8 %fusion.40 = f32[48,128,128]{2,0,1:T(8,128)S(1)} fusion(f32[48,128,128]{2,0,1:T(8,128)S(1)} %copy-done, s32[64]{0:T(128)S(1)} %slice_bitcast_fusion.3, f32[8,8,128,128]{3,2,1,0:T(8,128)S(1)} %bitcast.83), kind=kOutput, calls=%fused_computation.14.clone.1 | convolution fusion | flops 604769280 | bytes 10486016 | tf_op jit(solution)/shard_map/while/body/eval_jaxpr/dot_general | solution.py:28
  411.4 2.1 select_bitcast_fusion.3
  413.6 44.1 %all-reduce.5.cloned.1.call-done = f32[12,128,128]{2,1,0:T(8,128)} async-done(((f32[12,128,128]{2,1,0:T(8,128)}), f32[12,128,128]{2,1,0:T(8,128)}) %all-reduce.5.cloned.1.call-update) | async-done | bytes 786448 | tf_op jit(solution)/shard_map/while/body/eval_jaxpr/psum | solution.py:11
  457.7 3.9 gather_fusion.1
  461.6 2.8 gather_fusion
  464.3 7.2 %fusion.39 = f32[64,128,128]{2,1,0:T(8,128)S(1)} fusion(f32[64,128,128]{2,1,0:T(8,128)} %gather_fusion, f32[64,128,128]{2,1,0:T(8,128)} %gather_fusion.1, pred[64]{0:T(512)(128)(4,1)S(1)} %get-tuple-element.267, pred[64]{0:T(512)(128)(4,1)S(1)} %get-tuple-element.268), kind=kOutput, calls=%fused_computation.8.clone.1 | convolution fusion | flops 1612709888 | bytes 12583040 | tf_op jit(solution)/shard_map/while/body/eval_jaxpr/pij,pjk->pik/dot_general | solution.py:23
  471.6 5.8 %fusion.40 = f32[48,128,128]{2,0,1:T(8,128)S(1)} fusion(f32[48,128,128]{2,0,1:T(8,128)S(1)} %copy-done, s32[64]{0:T(128)S(1)} %slice_bitcast_fusion.3, f32[8,8,128,128]{3,2,1,0:T(8,128)S(1)} %bitcast.83), kind=kOutput, calls=%fused_computation.14.clone.1 | convolution fusion | flops 604769280 | bytes 10486016 | tf_op jit(solution)/shard_map/while/body/eval_jaxpr/dot_general | solution.py:28
  481.3 44.1 %all-reduce.5.cloned.1.call-done = f32[12,128,128]{2,1,0:T(8,128)} async-done(((f32[12,128,128]{2,1,0:T(8,128)}), f32[12,128,128]{2,1,0:T(8,128)}) %all-reduce.5.cloned.1.call-update) | async-done | bytes 786448 | tf_op jit(solution)/shard_map/while/body/eval_jaxpr/psum | solution.py:11
  525.4 3.9 gather_fusion.1
  529.3 2.8 gather_fusion
  532.1 7.2 %fusion.39 = f32[64,128,128]{2,1,0:T(8,128)S(1)} fusion(f32[64,128,128]{2,1,0:T(8,128)} %gather_fusion, f32[64,128,128]{2,1,0:T(8,128)} %gather_fusion.1, pred[64]{0:T(512)(128)(4,1)S(1)} %get-tuple-element.267, pred[64]{0:T(512)(128)(4,1)S(1)} %get-tuple-element.268), kind=kOutput, calls=%fused_computation.8.clone.1 | convolution fusion | flops 1612709888 | bytes 12583040 | tf_op jit(solution)/shard_map/while/body/eval_jaxpr/pij,pjk->pik/dot_general | solution.py:23
  539.3 5.8 %fusion.40 = f32[48,128,128]{2,0,1:T(8,128)S(1)} fusion(f32[48,128,128]{2,0,1:T(8,128)S(1)} %copy-done, s32[64]{0:T(128)S(1)} %slice_bitcast_fusion.3, f32[8,8,128,128]{3,2,1,0:T(8,128)S(1)} %bitcast.83), kind=kOutput, calls=%fused_computation.14.clone.1 | convolution fusion | flops 604769280 | bytes 10486016 | tf_op jit(solution)/shard_map/while/body/eval_jaxpr/dot_general | solution.py:28
  546.9 4.6 copy.34
  (104 shorter events, 17.9 us)
Async XLA Ops:
  6.5 3.4 copy-start.2
  6.5 49.9 %all-reduce.3.cloned.1.call-start = ((), (), s32[]{:S(2)}) async-start(), calls=%async_computation | async-start | bytes 1572864 | tf_op jit(solution)/shard_map/psum | solution.py:11
  73.7 46.2 %all-reduce.5.cloned.1.call-start = ((), (), s32[]{:S(2)}) async-start(), calls=%async_computation.1 | async-start | bytes 1572864 | tf_op jit(solution)/shard_map/while/body/eval_jaxpr/psum | solution.py:11
  73.7 50.1 %collective-permute-start = (f32[20,128,128]{2,1,0:T(8,128)S(1)}, f32[20,128,128]{2,1,0:T(8,128)S(1)}, u32[]{:S(2)}, u32[]{:S(2)}) collective-permute-start(f32[20,128,128]{2,1,0:T(8,128)S(1)} %get-tuple-element.284), channel_id=1, source_target_pairs={{0,4},{4,8},{8,12},{12,16},{16,20},{20,24},{24,28},{28,0},{1,5},{5... | collective-permute-start | bytes 3932168 | tf_op jit(solution)/shard_map/while/body/eval_jaxpr/ppermute | solution.py:17
  126.6 7.2 %copy-start = (f32[48,128,128]{2,0,1:T(8,128)S(1)}, f32[48,128,128]{2,0,1:T(8,128)}, u32[]{:S(2)}) copy-start(f32[48,128,128]{2,0,1:T(8,128)} %get-tuple-element.283) | copy-start | bytes 9437188 | tf_op jit(solution)/shard_map/while
  139.7 1.7 copy-start.1
  141.4 46.2 %all-reduce.5.cloned.1.call-start = ((), (), s32[]{:S(2)}) async-start(), calls=%async_computation.1 | async-start | bytes 1572864 | tf_op jit(solution)/shard_map/while/body/eval_jaxpr/psum | solution.py:11
  141.4 50.1 %collective-permute-start = (f32[20,128,128]{2,1,0:T(8,128)S(1)}, f32[20,128,128]{2,1,0:T(8,128)S(1)}, u32[]{:S(2)}, u32[]{:S(2)}) collective-permute-start(f32[20,128,128]{2,1,0:T(8,128)S(1)} %get-tuple-element.284), channel_id=1, source_target_pairs={{0,4},{4,8},{8,12},{12,16},{16,20},{20,24},{24,28},{28,0},{1,5},{5... | collective-permute-start | bytes 3932168 | tf_op jit(solution)/shard_map/while/body/eval_jaxpr/ppermute | solution.py:17
  194.4 7.2 %copy-start = (f32[48,128,128]{2,0,1:T(8,128)S(1)}, f32[48,128,128]{2,0,1:T(8,128)}, u32[]{:S(2)}) copy-start(f32[48,128,128]{2,0,1:T(8,128)} %get-tuple-element.283) | copy-start | bytes 9437188 | tf_op jit(solution)/shard_map/while
  207.4 1.7 copy-start.1
  209.2 45.9 %all-reduce.5.cloned.1.call-start = ((), (), s32[]{:S(2)}) async-start(), calls=%async_computation.1 | async-start | bytes 1572864 | tf_op jit(solution)/shard_map/while/body/eval_jaxpr/psum | solution.py:11
  209.2 49.8 %collective-permute-start = (f32[20,128,128]{2,1,0:T(8,128)S(1)}, f32[20,128,128]{2,1,0:T(8,128)S(1)}, u32[]{:S(2)}, u32[]{:S(2)}) collective-permute-start(f32[20,128,128]{2,1,0:T(8,128)S(1)} %get-tuple-element.284), channel_id=1, source_target_pairs={{0,4},{4,8},{8,12},{12,16},{16,20},{20,24},{24,28},{28,0},{1,5},{5... | collective-permute-start | bytes 3932168 | tf_op jit(solution)/shard_map/while/body/eval_jaxpr/ppermute | solution.py:17
  261.8 7.2 %copy-start = (f32[48,128,128]{2,0,1:T(8,128)S(1)}, f32[48,128,128]{2,0,1:T(8,128)}, u32[]{:S(2)}) copy-start(f32[48,128,128]{2,0,1:T(8,128)} %get-tuple-element.283) | copy-start | bytes 9437188 | tf_op jit(solution)/shard_map/while
  274.9 1.7 copy-start.1
  276.6 45.9 %all-reduce.5.cloned.1.call-start = ((), (), s32[]{:S(2)}) async-start(), calls=%async_computation.1 | async-start | bytes 1572864 | tf_op jit(solution)/shard_map/while/body/eval_jaxpr/psum | solution.py:11
  276.6 49.8 %collective-permute-start = (f32[20,128,128]{2,1,0:T(8,128)S(1)}, f32[20,128,128]{2,1,0:T(8,128)S(1)}, u32[]{:S(2)}, u32[]{:S(2)}) collective-permute-start(f32[20,128,128]{2,1,0:T(8,128)S(1)} %get-tuple-element.284), channel_id=1, source_target_pairs={{0,4},{4,8},{8,12},{12,16},{16,20},{20,24},{24,28},{28,0},{1,5},{5... | collective-permute-start | bytes 3932168 | tf_op jit(solution)/shard_map/while/body/eval_jaxpr/ppermute | solution.py:17
  329.2 7.2 %copy-start = (f32[48,128,128]{2,0,1:T(8,128)S(1)}, f32[48,128,128]{2,0,1:T(8,128)}, u32[]{:S(2)}) copy-start(f32[48,128,128]{2,0,1:T(8,128)} %get-tuple-element.283) | copy-start | bytes 9437188 | tf_op jit(solution)/shard_map/while
  342.3 1.7 copy-start.1
  344.0 45.9 %all-reduce.5.cloned.1.call-start = ((), (), s32[]{:S(2)}) async-start(), calls=%async_computation.1 | async-start | bytes 1572864 | tf_op jit(solution)/shard_map/while/body/eval_jaxpr/psum | solution.py:11
  344.0 49.8 %collective-permute-start = (f32[20,128,128]{2,1,0:T(8,128)S(1)}, f32[20,128,128]{2,1,0:T(8,128)S(1)}, u32[]{:S(2)}, u32[]{:S(2)}) collective-permute-start(f32[20,128,128]{2,1,0:T(8,128)S(1)} %get-tuple-element.284), channel_id=1, source_target_pairs={{0,4},{4,8},{8,12},{12,16},{16,20},{20,24},{24,28},{28,0},{1,5},{5... | collective-permute-start | bytes 3932168 | tf_op jit(solution)/shard_map/while/body/eval_jaxpr/ppermute | solution.py:17
  396.6 7.2 %copy-start = (f32[48,128,128]{2,0,1:T(8,128)S(1)}, f32[48,128,128]{2,0,1:T(8,128)}, u32[]{:S(2)}) copy-start(f32[48,128,128]{2,0,1:T(8,128)} %get-tuple-element.283) | copy-start | bytes 9437188 | tf_op jit(solution)/shard_map/while
  409.7 1.7 copy-start.1
  411.4 46.2 %all-reduce.5.cloned.1.call-start = ((), (), s32[]{:S(2)}) async-start(), calls=%async_computation.1 | async-start | bytes 1572864 | tf_op jit(solution)/shard_map/while/body/eval_jaxpr/psum | solution.py:11
  411.4 50.1 %collective-permute-start = (f32[20,128,128]{2,1,0:T(8,128)S(1)}, f32[20,128,128]{2,1,0:T(8,128)S(1)}, u32[]{:S(2)}, u32[]{:S(2)}) collective-permute-start(f32[20,128,128]{2,1,0:T(8,128)S(1)} %get-tuple-element.284), channel_id=1, source_target_pairs={{0,4},{4,8},{8,12},{12,16},{16,20},{20,24},{24,28},{28,0},{1,5},{5... | collective-permute-start | bytes 3932168 | tf_op jit(solution)/shard_map/while/body/eval_jaxpr/ppermute | solution.py:17
  464.3 7.2 %copy-start = (f32[48,128,128]{2,0,1:T(8,128)S(1)}, f32[48,128,128]{2,0,1:T(8,128)}, u32[]{:S(2)}) copy-start(f32[48,128,128]{2,0,1:T(8,128)} %get-tuple-element.283) | copy-start | bytes 9437188 | tf_op jit(solution)/shard_map/while
  477.4 1.7 copy-start.1
  479.2 46.2 %all-reduce.5.cloned.1.call-start = ((), (), s32[]{:S(2)}) async-start(), calls=%async_computation.1 | async-start | bytes 1572864 | tf_op jit(solution)/shard_map/while/body/eval_jaxpr/psum | solution.py:11
  479.2 50.1 %collective-permute-start = (f32[20,128,128]{2,1,0:T(8,128)S(1)}, f32[20,128,128]{2,1,0:T(8,128)S(1)}, u32[]{:S(2)}, u32[]{:S(2)}) collective-permute-start(f32[20,128,128]{2,1,0:T(8,128)S(1)} %get-tuple-element.284), channel_id=1, source_target_pairs={{0,4},{4,8},{8,12},{12,16},{16,20},{20,24},{24,28},{28,0},{1,5},{5... | collective-permute-start | bytes 3932168 | tf_op jit(solution)/shard_map/while/body/eval_jaxpr/ppermute | solution.py:17
  532.1 7.2 %copy-start = (f32[48,128,128]{2,0,1:T(8,128)S(1)}, f32[48,128,128]{2,0,1:T(8,128)}, u32[]{:S(2)}) copy-start(f32[48,128,128]{2,0,1:T(8,128)} %get-tuple-element.283) | copy-start | bytes 9437188 | tf_op jit(solution)/shard_map/while
  545.2 1.7 copy-start.1
Sparse Core Ops, SparseCore 0:
  10.1 46.3 all-reduce.2
  76.9 42.9 all-reduce.4
  144.6 42.9 all-reduce.4
  212.0 42.9 all-reduce.4
  279.5 42.9 all-reduce.4
  346.9 42.9 all-reduce.4
  414.6 42.9 all-reduce.4
  482.4 42.9 all-reduce.4
where the time goes:
time: 559 us; the launch traced here: 558 us
  waiting for transfers between devices  351 us (63%)
  matrix products  105 us (19%)
  local copies, waits for them, and re-layouts  71.5 us (13%)
  other arithmetic  16.7 us (3%)
  between operations  13.4 us (2%)
    psum x8, waiting for transfers between devices, spread(): return lax.psum(block, axis)  351 us
    dot_general x8, matrix products, apply_panel(): jnp.einsum('pij,pjk->pik', left_sel, right_sel, precision=lax.Precision.H...  57.7 us
    dot_general x8, matrix products, apply_panel(): jnp.dot(onehot, terms.reshape(count, -1), precision=lax.Precision.HIGHEST)  47 us
    gather x8, local copies, waits for them, and re-layouts, apply_panel(): left_sel = jnp.take(left, entries[:, 0], axis=0)  31.2 us
    gather x8, local copies, waits for them, and re-layouts, apply_panel(): right_sel = jnp.take(right, entries[:, 1], axis=0)  22.3 us
    select_n x8, other arithmetic, spread(): jnp.where(lax.axis_index(axis) == source, block, jnp.zeros_like(block))  16.6 us
    while x35, local copies, waits for them, and re-layouts  12 us
  transfers between devices with their start and end apart: 15, of which 8 were waited for; matrix products, arithmetic and copies ran while one was open for 8% of the time, Pallas kernels for 0%

commit v1 on v0

v1 whole, which is shorter than its diff:
```python
import functools

import jax
import jax.numpy as jnp
from jax import lax
from jax.experimental import pallas as pl
from jax.experimental.pallas import tpu as pltpu
from jax.sharding import PartitionSpec as P

SC = 48
GROUP = 16
F32, BF16 = jnp.float32, jnp.bfloat16


def along(value, axis, pairs):
    return lax.ppermute(value, axis, pairs)


def rows_by_distance(own, count):
    half = own.shape[0] // 2
    swap = lambda v, bit: along(v, "row", [(i, i ^ bit) for i in range(count)])
    held = {0: [own]}
    bits = [1 << i for i in range(count.bit_length()) if 1 < (1 << i) < count]
    whole = {0: own}
    for bit in bits:
        whole[bit] = swap(own, bit)
        held[bit] = [whole[bit]]
    halves = {m: (whole[m][:half], whole[m][half:]) for m in whole}
    for mask in range(2, count, 2):
        if mask in halves:
            continue
        low, high = mask & -mask, 1 << (mask.bit_length() - 1)
        halves[mask] = (swap(halves[mask ^ high][0], high), swap(halves[mask ^ low][1], low))
        held[mask] = list(halves[mask])
    for mask in list(held):
        held[mask | 1] = [swap(piece, 1) for piece in held[mask]]
    return [held[mask] for mask in range(count)]


def split(x):
    high = x.astype(BF16)
    return high, (x - high.astype(F32)).astype(BF16)


def product(left, right):
    both = jnp.dot(left, jnp.concatenate([right, right], 0), preferred_element_type=F32)
    n = both.shape[1] // 2
    return both[:, :n] + both[:, n:]


def split_into(source, target, base):
    n = source.shape[-1]

    @pl.loop(0, source.shape[0])
    def _(i):
        high, low = split(source[i])
        target[base + i, :, :n] = high
        target[base + i, :, n:] = low


def add_products(meta, lists, a_split, b_split, acc, sources, a_slots, b_slots, per_list, b_base):
    @pl.loop(0, sources)
    def _(t):
        panel, count = meta[3 * t], meta[3 * t + 1]
        b_at = b_base(t) * b_slots

        @pl.loop(0, (count + GROUP - 1) // GROUP)
        def _(g):
            terms, slots = [], []
            for u in range(GROUP):
                entry = lists[panel * per_list + g * GROUP + u]
                slots.append(entry & 1023)
                right = b_split[b_at + ((entry >> 10) & 1023)]
                left = a_split[t * a_slots + (entry >> 20)]
                terms.append(product(left, right))
            for slot, term in zip(slots, terms):
                acc[slot] += term


def first_kernel(sources, pieces, per_list, *refs):
    meta, lists = refs[:2]
    a_refs = refs[2 : 2 + sources]
    b_refs = refs[2 + sources : 2 + sources + len(pieces)]
    acc_out, b_out, a_buf, b_buf, a_split, b_split, acc, sem = refs[2 + sources + len(pieces) :]
    a_slots = a_refs[0].shape[0]
    b_slots = b_split.shape[0] // (1 + max(code for code, _ in pieces))
    copies = []
    for t in range(sources):
        copies.append((pltpu.make_async_copy(a_refs[t], a_buf.at[pl.ds(t * a_slots, a_slots)], sem.at[t]), t * a_slots, a_slots))
    b_copies = []
    for j, (code, offset) in enumerate(pieces):
        n, at = b_refs[j].shape[0], code * b_slots + offset
        b_copies.append((pltpu.make_async_copy(b_refs[j], b_buf.at[pl.ds(at, n)], sem.at[sources + j]), at, n))
    for copy, _, _ in copies + b_copies:
        copy.start()
    acc[...] = jnp.zeros_like(acc)
    for copy, at, n in copies:
        copy.wait()
        split_into(a_buf.at[pl.ds(at, n)], a_split, at)
    for copy, at, n in b_copies:
        copy.wait()
        split_into(b_buf.at[pl.ds(at, n)], b_split, at)
    keep = pltpu.make_async_copy(b_split, b_out, sem.at[0])
    keep.start()
    add_products(
        meta, lists, a_split, b_split, acc, sources, a_slots, b_slots, per_list, lambda t: meta[3 * t + 2]
    )
    done = pltpu.make_async_copy(acc.at[pl.ds(0, SC)], acc_out, sem.at[1])
    done.start()
    keep.wait()
    done.wait()


def later_kernel(sources, per_list, *refs):
    meta, lists = refs[:2]
    a_refs = refs[2 : 2 + sources]
    b_in, acc_in, acc_out, a_buf, a_split, b_split, acc, sem = refs[2 + sources :]
    a_slots = a_refs[0].shape[0]
    b_slots = b_split.shape[0] // sources
    load = pltpu.make_async_copy(acc_in, acc.at[pl.ds(0, SC)], sem.at[0])
    load.start()

    def copies(t):
        b_at = meta[3 * t + 2] * b_slots
        return (
            pltpu.make_async_copy(a_refs[t], a_buf.at[pl.ds(t * a_slots, a_slots)], sem.at[1 + 2 * t]),
            pltpu.make_async_copy(
                b_in.at[pl.ds(b_at, b_slots)], b_split.at[pl.ds(t * b_slots, b_slots)], sem.at[2 + 2 * t]
            ),
        )

    for t in range(sources):

        @pl.when(meta[3 * t + 1] > 0)
        def _():
            for copy in copies(t):
                copy.start()

    for t in range(sources):

        @pl.when(meta[3 * t + 1] > 0)
        def _():
            a_copy, b_copy = copies(t)
            a_copy.wait()
            split_into(a_buf.at[pl.ds(t * a_slots, a_slots)], a_split, t * a_slots)
            b_copy.wait()

    load.wait()
    add_products(meta, lists, a_split, b_split, acc, sources, a_slots, b_slots, per_list, lambda t: t)
    done = pltpu.make_async_copy(acc.at[pl.ds(0, SC)], acc_out, sem.at[0])
    done.start()
    done.wait()


ANY = pl.BlockSpec(memory_space=pl.ANY)
SMEM = pl.BlockSpec(memory_space=pltpu.SMEM)


def run_first(meta, lists, a_list, b_held, per_list):
    a_slots, size, _ = a_list[0].shape
    sources, codes = len(a_list), len(b_held)
    b_slots = sum(piece.shape[0] for piece in b_held[0])
    pieces, arrays = [], []
    for code, parts in enumerate(b_held):
        offset = 0
        for part in parts:
            pieces.append((code, offset))
            arrays.append(part)
            offset += part.shape[0]
    work = sources * per_list * 2 * size**3 * 4
    return pl.pallas_call(
        functools.partial(first_kernel, sources, tuple(pieces), per_list),
        out_shape=(
            jax.ShapeDtypeStruct((SC, size, size), F32),
            jax.ShapeDtypeStruct((codes * b_slots, size, 2 * size), BF16),
        ),
        in_specs=[SMEM, SMEM] + [ANY] * (sources + len(arrays)),
        out_specs=(ANY, ANY),
        scratch_shapes=[
            pltpu.VMEM((sources * a_slots, size, size), F32),
            pltpu.VMEM((codes * b_slots, size, size), F32),
            pltpu.VMEM((sources * a_slots, size, 2 * size), BF16),
            pltpu.VMEM((codes * b_slots, size, 2 * size), BF16),
            pltpu.VMEM((SC + 1, size, size), F32),
            pltpu.SemaphoreType.DMA((sources + len(arrays),)),
        ],
        compiler_params=pltpu.CompilerParams(vmem_limit_bytes=56 << 20),
        cost_estimate=pl.CostEstimate(flops=work, bytes_accessed=40 << 20, transcendentals=0),
        name="first_panels",
    )(meta, lists, *a_list, *arrays)


def run_later(meta, lists, a_list, b_all, acc, codes, per_list):
    a_slots, size, _ = a_list[0].shape
    sources = len(a_list)
    b_slots = b_all.shape[0] // codes
    work = per_list * 2 * size**3 * 4 * sources // 2
    return pl.pallas_call(
        functools.partial(later_kernel, sources, per_list),
        out_shape=jax.ShapeDtypeStruct(acc.shape, F32),
        in_specs=[SMEM, SMEM] + [ANY] * (sources + 2),
        out_specs=ANY,
        scratch_shapes=[
            pltpu.VMEM((sources * a_slots, size, size), F32),
            pltpu.VMEM((sources * a_slots, size, 2 * size), BF16),
            pltpu.VMEM((sources * b_slots, size, 2 * size), BF16),
            pltpu.VMEM((SC + 1, size, size), F32),
            pltpu.SemaphoreType.DMA((1 + 2 * sources,)),
        ],
        compiler_params=pltpu.CompilerParams(vmem_limit_bytes=24 << 20),
        cost_estimate=pl.CostEstimate(flops=work, bytes_accessed=16 << 20, transcendentals=0),
        name="later_panels",
    )(meta, lists, *a_list, b_all, acc)


def on_device(cols, rows, a_blocks, b_blocks, product_lists):
    row, col = lax.axis_index("row"), lax.axis_index("col")
    own = a_blocks[0]
    per_device = own.shape[0]
    entries = product_lists[0, 0]
    per_list = -(-entries.shape[1] // GROUP) * GROUP
    entries = jnp.pad(entries, ((0, 0), (0, per_list - entries.shape[1]), (0, 0)), constant_values=SC)
    real = entries[:, :, 2] < SC
    counts = jnp.sum(real.astype(jnp.int32), axis=1)
    packed = jnp.where(real, (entries[:, :, 0] << 20) | (entries[:, :, 1] << 10) | entries[:, :, 2], SC)
    packed = packed.reshape(-1)

    def meta_of(sources):
        out = []
        for holder, q in sources:
            valid = (holder >= 0) & (holder < cols)
            panel = jnp.where(valid, holder * per_device + q, 0)
            count = jnp.where(valid, lax.dynamic_index_in_dim(counts, panel, 0, keepdims=False), 0)
            out += [panel, count, panel ^ row]
        return jnp.stack(out).astype(jnp.int32)

    arrived = []
    for q in range(per_device):
        right = left = own[q]
        steps = [[(own[q], (col, q))]]
        for s in range(1, cols):
            right = along(right, "col", [(i, i + 1) for i in range(s - 1, cols - 1)])
            left = along(left, "col", [(i, i - 1) for i in range(1, cols - s + 1)])
            steps.append([(right, (col - s, q)), (left, (col + s, q))])
        arrived.append(steps)

    b_held = rows_by_distance(b_blocks[0, 0], rows)

    early = [item for s in range(min(2, cols)) for q in range(per_device) for item in arrived[q][s]]
    acc, b_all = run_first(meta_of([m for _, m in early]), packed, [a for a, _ in early], b_held, per_list)
    for s in range(2, cols):
        if s < cols - 1:
            stages = [[item for q in range(per_device) for item in arrived[q][s]]]
        else:
            stages = [arrived[q][s] for q in range(per_device)]
        for items in stages:
            acc = run_later(
                meta_of([m for _, m in items]), packed, [a for a, _ in items], b_all, acc, rows, per_list
            )
    return acc.reshape((1, 1) + acc.shape)


def solution(mesh):
    spec = P("row", "col", None, None, None)
    return jax.shard_map(
        functools.partial(on_device, mesh.shape["col"], mesh.shape["row"]),
        mesh=mesh,
        in_specs=(spec, spec, spec),
        out_specs=spec,
        check_vma=False,
    )
```

time: 559 us -> 146 us (0.26)
  waiting for transfers between devices: 351 us -> 71.4 us
  matrix products: 105 us -> 0 us
  local copies, waits for them, and re-layouts: 71.5 us -> 12 us
  starting transfers between devices: 0.04 us -> 26.3 us
  Pallas kernels: 0 us -> 25.8 us
  other arithmetic: 16.7 us -> 0.12 us
    psum x8 -> x0, waiting for transfers between devices: 351 us -> none  [spread(): return lax.psum(block, axis)]
    dot_general x16 -> x0, matrix products: 105 us -> none  [the longest x8 57.7 us: apply_panel(): jnp.einsum('pij,pjk->pik', left_sel, right_sel, precision=lax.Precision.H...]
    ppermute x7 -> x21, waiting for transfers between devices: 0.02 us -> 71.4 us  [along(): return lax.ppermute(value, axis, pairs)]
    gather x16 -> x0, local copies, waits for them, and re-layouts: 53.5 us -> none  [the longest x8 31.2 us: apply_panel(): left_sel = jnp.take(left, entries[:, 0], axis=0)]
    ppermute x7 -> x21, starting transfers between devices: 0.02 us -> 26.3 us  [along(): return lax.ppermute(value, axis, pairs)]
    pallas_call x0 -> x4, Pallas kernels: none -> 25.8 us  [the longest x1 14.1 us: run_first(): pl.pallas_call(functools.partial(first_kernel, sources, tuple(pieces), pe...]
    select_n x8 -> x1, other arithmetic: 16.6 us -> 0.01 us  [on_device(): jnp.where(real, entries[:, :, 0] << 20 | entries[:, :, 1] << 10 | entries...]
    while x36 -> x0, local copies, waits for them, and re-layouts: 16.6 us -> none
  transfers between devices with their start and end apart: 15 -> 21, of which waited for: 8 -> 6; matrix products, arithmetic and copies ran while one was open for 8% -> 3% of each run, Pallas kernels for 0% -> 15%
where the time goes in v1:
time: 146 us; the launch traced here: 145 us
  waiting for transfers between devices  71.4 us (49%)
  starting transfers between devices  26.3 us (18%)
  Pallas kernels  25.8 us (18%)
  local copies, waits for them, and re-layouts  12 us (8%)
  between operations  8.99 us (6%)
    ppermute x21, waiting for transfers between devices, along(): return lax.ppermute(value, axis, pairs)  71.4 us
    ppermute x21, starting transfers between devices, along(): return lax.ppermute(value, axis, pairs)  26.3 us
    pallas_call x1, Pallas kernels, run_first(): pl.pallas_call(functools.partial(first_kernel, sources, tuple(pieces), pe...  14.1 us
    pallas_call x3, Pallas kernels, run_later(): pl.pallas_call(functools.partial(later_kernel, sources, per_list), out_sh...  11.6 us
    unnamed x24, local copies, waits for them, and re-layouts  5.9 us
  transfers between devices with their start and end apart: 21, of which 6 were waited for; matrix products, arithmetic and copies ran while one was open for 3% of the time, Pallas kernels for 15%

profile of v1, /device:TPU:0, one launch (start us, length us, event | category | flops | bytes accessed | tf_op | source)
XLA Modules:
  0.0 144.6 jit_solution(396424503118407397)
XLA Ops:
  0.0 1.6 %slice_bitcast_fusion = (f32[12,128,128]{2,1,0:T(8,128)S(1)}, f32[12,128,128]{2,1,0:T(8,128)S(1)}) fusion(f32[1,2,12,128,128]{4,3,2,1,0:T(8,128)} %param.3), kind=kLoop, calls=%fused_computation | loop fusion | bytes 3145728 | tf_op jit(solution)/shard_map/squeeze | solution.py:240
  1.6 0.0 copy-start.6
  1.6 5.1 %collective-permute-start = (f32[12,128,128]{2,1,0:T(8,128)S(1)}, f32[12,128,128]{2,1,0:T(8,128)S(1)}, u32[]{:S(2)}, u32[]{:S(2)}) collective-permute-start(f32[12,128,128]{2,1,0:T(8,128)S(1)} %get-tuple-element.12.refs_3_), channel_id=1, source_target_pairs={{0,1},{1,2},{2,3},{4,5},{5,6},{6,7},{8,9},{9,10},{10,11},{12,13},{... | collective-permute-start | bytes 2359304 | tf_op jit(solution)/shard_map/ppermute | solution.py:16
  6.7 1.6 %collective-permute-start.9 = (f32[20,128,128]{2,1,0:T(8,128)S(1)}, f32[20,128,128]{2,1,0:T(8,128)}, u32[]{:S(2)}, u32[]{:S(2)}) collective-permute-start(f32[20,128,128]{2,1,0:T(8,128)S(1)} %bitcast.67), channel_id=1, source_target_pairs={{0,8},{4,12},{8,0},{12,4},{16,24},{20,28},{24,16},{28,20},{1,9},{5... | collective-permute-start | bytes 3932168 | tf_op jit(solution)/shard_map/ppermute | solution.py:16
  8.3 1.5 %collective-permute-start.11 = (f32[20,128,128]{2,1,0:T(8,128)S(1)}, f32[20,128,128]{2,1,0:T(8,128)}, u32[]{:S(2)}, u32[]{:S(2)}) collective-permute-start(f32[20,128,128]{2,1,0:T(8,128)S(1)} %bitcast.68), channel_id=1, source_target_pairs={{0,16},{4,20},{8,24},{12,28},{16,0},{20,4},{24,8},{28,12},{1,17},{... | collective-permute-start | bytes 3932168 | tf_op jit(solution)/shard_map/ppermute | solution.py:16
  9.8 3.5 %collective-permute-start.6 = (f32[12,128,128]{2,1,0:T(8,128)S(1)}, f32[12,128,128]{2,1,0:T(8,128)S(1)}, u32[]{:S(2)}, u32[]{:S(2)}) collective-permute-start(f32[12,128,128]{2,1,0:T(8,128)S(1)} %get-tuple-element.11.refs_2_), channel_id=1, source_target_pairs={{0,1},{1,2},{2,3},{4,5},{5,6},{6,7},{8,9},{9,10},{10,11},{12,13},{... | collective-permute-start | bytes 2359304 | tf_op jit(solution)/shard_map/ppermute | solution.py:16
  13.3 1.3 collective-permute-start.7
  14.6 10.0 %collective-permute-done.refs_6_ = f32[12,128,128]{2,1,0:T(8,128)S(1)} collective-permute-done((f32[12,128,128]{2,1,0:T(8,128)S(1)}, f32[12,128,128]{2,1,0:T(8,128)S(1)}, u32[]{:S(2)}, u32[]{:S(2)}) %collective-permute-start) | collective-permute-done | bytes 786464 | tf_op jit(solution)/shard_map/ppermute | solution.py:16
  24.6 15.7 %collective-permute-done.6.refs_4_ = f32[12,128,128]{2,1,0:T(8,128)S(1)} collective-permute-done((f32[12,128,128]{2,1,0:T(8,128)S(1)}, f32[12,128,128]{2,1,0:T(8,128)S(1)}, u32[]{:S(2)}, u32[]{:S(2)}) %collective-permute-start.6) | collective-permute-done | bytes 786464 | tf_op jit(solution)/shard_map/ppermute | solution.py:16
  40.3 1.3 collective-permute-start.3
  41.6 0.0 collective-permute-done.7.refs_5_
  41.6 0.7 collective-permute-start.1
  42.4 0.7 collective-permute-start.17
  43.1 1.3 collective-permute-start.19
  44.4 1.1 slice.36
  45.5 1.1 slice.37
  46.7 16.6 %collective-permute-done.3.refs_7_ = f32[12,128,128]{2,1,0:T(8,128)} collective-permute-done((f32[12,128,128]{2,1,0:T(8,128)S(1)}, f32[12,128,128]{2,1,0:T(8,128)}, u32[]{:S(2)}, u32[]{:S(2)}) %collective-permute-start.3) | collective-permute-done | bytes 786464 | tf_op jit(solution)/shard_map/ppermute | solution.py:16
  63.3 1.5 %collective-permute-start.13 = (f32[10,128,128]{2,1,0:T(8,128)S(1)}, f32[10,128,128]{2,1,0:T(8,128)}, u32[]{:S(2)}, u32[]{:S(2)}) collective-permute-start(f32[10,128,128]{2,1,0:T(8,128)S(1)} %slice.36), channel_id=1, source_target_pairs={{0,16},{4,20},{8,24},{12,28},{16,0},{20,4},{24,8},{28,12},{1,17},{... | collective-permute-start | bytes 1966088 | tf_op jit(solution)/shard_map/ppermute | solution.py:16
  64.8 0.0 collective-permute-done.8.refs_9_
  64.8 1.5 %collective-permute-start.14 = (f32[10,128,128]{2,1,0:T(8,128)S(1)}, f32[10,128,128]{2,1,0:T(8,128)}, u32[]{:S(2)}, u32[]{:S(2)}) collective-permute-start(f32[10,128,128]{2,1,0:T(8,128)S(1)} %slice.37), channel_id=1, source_target_pairs={{0,8},{4,12},{8,0},{12,4},{16,24},{20,28},{24,16},{28,20},{1,9},{5... | collective-permute-start | bytes 1966088 | tf_op jit(solution)/shard_map/ppermute | solution.py:16
  66.3 0.0 collective-permute-done.1.refs_4_
  66.3 0.0 collective-permute-start.10
  66.3 0.0 collective-permute-done.17.refs_2_
  66.3 0.5 collective-permute-start.12
  66.8 11.4 %collective-permute-done.19.refs_3_ = f32[12,128,128]{2,1,0:T(8,128)S(1)} collective-permute-done((f32[12,128,128]{2,1,0:T(8,128)S(1)}, f32[12,128,128]{2,1,0:T(8,128)S(1)}, u32[]{:S(2)}, u32[]{:S(2)}) %collective-permute-start.19) | collective-permute-done | bytes 786464 | tf_op jit(solution)/shard_map/ppermute | solution.py:16
  78.2 1.3 collective-permute-start.4
  79.5 0.1 collective-permute-start.15
  79.6 0.0 collective-permute-done.14.refs_15_
  79.6 0.5 collective-permute-start.16
  80.1 0.1 convert_reduce_fusion
  80.2 0.7 fusion.3
  84.6 0.7 select_n.143.refs_1_
  90.3 0.1 stack.170.refs_0_
  90.3 0.1 stack.144.refs_0_
  90.4 0.1 stack.183.refs_0_
  90.5 0.6 stack.163.refs_0_
  91.1 10.4 %collective-permute-done.4.refs_5_ = f32[12,128,128]{2,1,0:T(8,128)S(1)} collective-permute-done((f32[12,128,128]{2,1,0:T(8,128)}, f32[12,128,128]{2,1,0:T(8,128)S(1)}, u32[]{:S(2)}, u32[]{:S(2)}) %collective-permute-start.4) | collective-permute-done | bytes 786464 | tf_op jit(solution)/shard_map/ppermute | solution.py:16
  101.5 0.7 collective-permute-start.18
  102.2 1.3 collective-permute-start.20
  103.5 0.7 collective-permute-start.2
  104.2 1.3 collective-permute-start.5
  105.6 14.1 %first_panels.1 = (f32[48,128,128]{2,1,0:T(8,128)}, bf16[160,128,256]{2,1,0:T(8,128)(2,1)}) custom-call(s32[18]{0:T(128)} %stack.163.refs_0_, s32[512]{0:T(512)} %select_n.143.refs_1_, f32[12,128,128]{2,1,0:T(8,128)} %copy-done.4, f32[12,128,128]{2,1,0:T(8,128)} %copy-done.5, f32[12,128,128]{2,1,0:T(8,128)} %copy-done.10, f32[12,128,128]{2,1,0:T(8,128)} %copy-done.11, ...), custom_call_target="tpu_custom_call" | custom-call | flops 6442450944 | bytes 41943040 | tf_op jit(solution)/shard_map/first_panels/pallas_call | solution.py:171
  119.7 4.0 %copy-done = bf16[160,128,256]{2,1,0:T(8,128)(2,1)S(1)} copy-done((bf16[160,128,256]{2,1,0:T(8,128)(2,1)S(1)}, bf16[160,128,256]{2,1,0:T(8,128)(2,1)}, u32[]{:S(2)}) %copy-start) | copy-done | bytes 10485784
  123.7 1.9 %copy-done.2 = f32[48,128,128]{2,1,0:T(8,128)S(1)} copy-done((f32[48,128,128]{2,1,0:T(8,128)S(1)}, f32[48,128,128]{2,1,0:T(8,128)}, u32[]{:S(2)}) %copy-start.2) | copy-done | bytes 3145752
  125.6 4.1 %later_panels.3.refs_5_ = f32[48,128,128]{2,1,0:T(8,128)S(1)} custom-call(s32[12]{0:T(128)S(1)} %stack.183.refs_0_, s32[512]{0:T(512)S(1)} %copy-done.3, f32[12,128,128]{2,1,0:T(8,128)S(1)} %collective-permute-done.17.refs_2_, f32[12,128,128]{2,1,0:T(8,128)S(1)} %collective-permute-done.19.refs_3_, f32[12,128,128]{2,1,0:T(8,128)S(1)} %collective-permute-done.1.refs_4_, ...), custom_call_target="tpu_custom_call" | custom-call | flops 2147483648 | bytes 16777216 | tf_op jit(solution)/shard_map/later_panels/pallas_call | solution.py:198
  129.7 3.3 %later_panels.4.refs_5_ = f32[48,128,128]{2,1,0:T(8,128)S(1)} custom-call(s32[6]{0:T(128)S(1)} %stack.170.refs_0_, s32[512]{0:T(512)S(1)} %copy-done.3, f32[12,128,128]{2,1,0:T(8,128)S(1)} %collective-permute-done.18.refs_2_, f32[12,128,128]{2,1,0:T(8,128)S(1)} %collective-permute-done.20.refs_3_, bf16[160,128,256]{2,1,0:T(8,128)(2,1)S(1)} %copy-done.1, ...), custom_call_target="tpu_custom_call" | custom-call | flops 1073741824 | bytes 16777216 | tf_op jit(solution)/shard_map/later_panels/pallas_call | solution.py:198
  133.0 7.3 %collective-permute-done.5.refs_3_ = f32[12,128,128]{2,1,0:T(8,128)S(1)} collective-permute-done((f32[12,128,128]{2,1,0:T(8,128)S(1)}, f32[12,128,128]{2,1,0:T(8,128)S(1)}, u32[]{:S(2)}, u32[]{:S(2)}) %collective-permute-start.5) | collective-permute-done | bytes 786464 | tf_op jit(solution)/shard_map/ppermute | solution.py:16
  140.3 4.2 %later_panels.5 = f32[48,128,128]{2,1,0:T(8,128)} custom-call(s32[6]{0:T(128)S(1)} %stack.144.refs_0_, s32[512]{0:T(512)S(1)} %copy-done.3, f32[12,128,128]{2,1,0:T(8,128)S(1)} %collective-permute-done.2.refs_2_, f32[12,128,128]{2,1,0:T(8,128)S(1)} %collective-permute-done.5.refs_3_, bf16[160,128,256]{2,1,0:T(8,128)(2,1)S(1)} %copy-done.1, ...), custom_call_target="tpu_custom_call" | custom-call | flops 1073741824 | bytes 16777216 | tf_op jit(solution)/shard_map/later_panels/pallas_call | solution.py:198
  (33 shorter events, 0.1 us)
Async XLA Ops:
  0.0 6.7 %copy-start.7 = (f32[1,1,20,128,128]{4,3,2,1,0:T(8,128)S(1)}, f32[1,1,20,128,128]{4,3,2,1,0:T(8,128)}, u32[]{:S(2)}) copy-start(f32[1,1,20,128,128]{4,3,2,1,0:T(8,128)} %param.4) | copy-start | bytes 3932164
  1.6 76.6 %copy-start.4 = (f32[12,128,128]{2,1,0:T(8,128)}, f32[12,128,128]{2,1,0:T(8,128)S(1)}, u32[]{:S(2)}) copy-start(f32[12,128,128]{2,1,0:T(8,128)S(1)} %get-tuple-element.11.refs_2_) | copy-start | bytes 2359300
  1.6 77.9 %copy-start.5 = (f32[12,128,128]{2,1,0:T(8,128)}, f32[12,128,128]{2,1,0:T(8,128)S(1)}, u32[]{:S(2)}) copy-start(f32[12,128,128]{2,1,0:T(8,128)S(1)} %get-tuple-element.12.refs_3_) | copy-start | bytes 2359300
  1.6 78.5 %copy-start.6 = (s32[1,1,8,64,3]{3,2,4,1,0:T(8,128)S(1)}, s32[1,1,8,64,3]{3,2,4,1,0:T(8,128)}, u32[]{:S(2)}) copy-start(s32[1,1,8,64,3]{3,2,4,1,0:T(8,128)} %param.5) | copy-start | bytes 18436
  1.6 23.0 %collective-permute-start = (f32[12,128,128]{2,1,0:T(8,128)S(1)}, f32[12,128,128]{2,1,0:T(8,128)S(1)}, u32[]{:S(2)}, u32[]{:S(2)}) collective-permute-start(f32[12,128,128]{2,1,0:T(8,128)S(1)} %get-tuple-element.12.refs_3_), channel_id=1, source_target_pairs={{0,1},{1,2},{2,3},{4,5},{5,6},{6,7},{8,9},{9,10},{10,11},{12,13},{... | collective-permute-start | bytes 2359304 | tf_op jit(solution)/shard_map/ppermute | solution.py:16
  6.7 35.6 %collective-permute-start.9 = (f32[20,128,128]{2,1,0:T(8,128)S(1)}, f32[20,128,128]{2,1,0:T(8,128)}, u32[]{:S(2)}, u32[]{:S(2)}) collective-permute-start(f32[20,128,128]{2,1,0:T(8,128)S(1)} %bitcast.67), channel_id=1, source_target_pairs={{0,8},{4,12},{8,0},{12,4},{16,24},{20,28},{24,16},{28,20},{1,9},{5... | collective-permute-start | bytes 3932168 | tf_op jit(solution)/shard_map/ppermute | solution.py:16
  8.3 34.8 %collective-permute-start.11 = (f32[20,128,128]{2,1,0:T(8,128)S(1)}, f32[20,128,128]{2,1,0:T(8,128)}, u32[]{:S(2)}, u32[]{:S(2)}) collective-permute-start(f32[20,128,128]{2,1,0:T(8,128)S(1)} %bitcast.68), channel_id=1, source_target_pairs={{0,16},{4,20},{8,24},{12,28},{16,0},{20,4},{24,8},{28,12},{1,17},{... | collective-permute-start | bytes 3932168 | tf_op jit(solution)/shard_map/ppermute | solution.py:16
  9.8 30.5 %collective-permute-start.6 = (f32[12,128,128]{2,1,0:T(8,128)S(1)}, f32[12,128,128]{2,1,0:T(8,128)S(1)}, u32[]{:S(2)}, u32[]{:S(2)}) collective-permute-start(f32[12,128,128]{2,1,0:T(8,128)S(1)} %get-tuple-element.11.refs_2_), channel_id=1, source_target_pairs={{0,1},{1,2},{2,3},{4,5},{5,6},{6,7},{8,9},{9,10},{10,11},{12,13},{... | collective-permute-start | bytes 2359304 | tf_op jit(solution)/shard_map/ppermute | solution.py:16
  13.3 28.3 %collective-permute-start.7 = (f32[12,128,128]{2,1,0:T(8,128)S(1)}, f32[12,128,128]{2,1,0:T(8,128)S(1)}, u32[]{:S(2)}, u32[]{:S(2)}) collective-permute-start(f32[12,128,128]{2,1,0:T(8,128)S(1)} %get-tuple-element.11.refs_2_), channel_id=1, source_target_pairs={{1,0},{2,1},{3,2},{5,4},{6,5},{7,6},{9,8},{10,9},{11,10},{13,12},{... | collective-permute-start | bytes 2359304 | tf_op jit(solution)/shard_map/ppermute | solution.py:16
  24.6 42.2 %copy-start.9 = (f32[12,128,128]{2,1,0:T(8,128)}, f32[12,128,128]{2,1,0:T(8,128)S(1)}, u32[]{:S(2)}) copy-start(f32[12,128,128]{2,1,0:T(8,128)S(1)} %collective-permute-done.refs_6_) | copy-start | bytes 2359300
  24.6 40.2 %collective-permute-start.8 = (f32[20,128,128]{2,1,0:T(8,128)S(1)}, f32[20,128,128]{2,1,0:T(8,128)S(1)}, u32[]{:S(2)}, u32[]{:S(2)}) collective-permute-start(f32[20,128,128]{2,1,0:T(8,128)S(1)} %bitcast.69), channel_id=1, source_target_pairs={{0,4},{4,0},{8,12},{12,8},{16,20},{20,16},{24,28},{28,24},{1,5},{5... | collective-permute-start | bytes 3932168 | tf_op jit(solution)/shard_map/ppermute | solution.py:16
  40.3 39.8 %copy-start.10 = (f32[12,128,128]{2,1,0:T(8,128)}, f32[12,128,128]{2,1,0:T(8,128)S(1)}, u32[]{:S(2)}) copy-start(f32[12,128,128]{2,1,0:T(8,128)S(1)} %collective-permute-done.6.refs_4_) | copy-start | bytes 2359300
  40.3 22.9 %collective-permute-start.3 = (f32[12,128,128]{2,1,0:T(8,128)S(1)}, f32[12,128,128]{2,1,0:T(8,128)}, u32[]{:S(2)}, u32[]{:S(2)}) collective-permute-start(f32[12,128,128]{2,1,0:T(8,128)S(1)} %get-tuple-element.12.refs_3_), channel_id=1, source_target_pairs={{1,0},{2,1},{3,2},{5,4},{6,5},{7,6},{9,8},{10,9},{11,10},{13,12},{... | collective-permute-start | bytes 2359304 | tf_op jit(solution)/shard_map/ppermute | solution.py:16
  41.6 38.5 %copy-start.11 = (f32[12,128,128]{2,1,0:T(8,128)}, f32[12,128,128]{2,1,0:T(8,128)S(1)}, u32[]{:S(2)}) copy-start(f32[12,128,128]{2,1,0:T(8,128)S(1)} %collective-permute-done.7.refs_5_) | copy-start | bytes 2359300
  41.6 24.6 %collective-permute-start.1 = (f32[12,128,128]{2,1,0:T(8,128)S(1)}, f32[12,128,128]{2,1,0:T(8,128)S(1)}, u32[]{:S(2)}, u32[]{:S(2)}) collective-permute-start(f32[12,128,128]{2,1,0:T(8,128)S(1)} %collective-permute-done.refs_6_), channel_id=1, source_target_pairs={{1,2},{2,3},{5,6},{6,7},{9,10},{10,11},{13,14},{14,15},{17,18},{18... | collective-permute-start | bytes 2359304 | tf_op jit(solution)/shard_map/ppermute | solution.py:16
  42.4 23.9 %collective-permute-start.17 = (f32[12,128,128]{2,1,0:T(8,128)S(1)}, f32[12,128,128]{2,1,0:T(8,128)S(1)}, u32[]{:S(2)}, u32[]{:S(2)}) collective-permute-start(f32[12,128,128]{2,1,0:T(8,128)S(1)} %collective-permute-done.6.refs_4_), channel_id=1, source_target_pairs={{1,2},{2,3},{5,6},{6,7},{9,10},{10,11},{13,14},{14,15},{17,18},{18... | collective-permute-start | bytes 2359304 | tf_op jit(solution)/shard_map/ppermute | solution.py:16
  43.1 35.1 %collective-permute-start.19 = (f32[12,128,128]{2,1,0:T(8,128)S(1)}, f32[12,128,128]{2,1,0:T(8,128)S(1)}, u32[]{:S(2)}, u32[]{:S(2)}) collective-permute-start(f32[12,128,128]{2,1,0:T(8,128)S(1)} %collective-permute-done.7.refs_5_), channel_id=1, source_target_pairs={{1,0},{2,1},{5,4},{6,5},{9,8},{10,9},{13,12},{14,13},{17,16},{18,1... | collective-permute-start | bytes 2359304 | tf_op jit(solution)/shard_map/ppermute | solution.py:16
  63.3 16.3 %collective-permute-start.13 = (f32[10,128,128]{2,1,0:T(8,128)S(1)}, f32[10,128,128]{2,1,0:T(8,128)}, u32[]{:S(2)}, u32[]{:S(2)}) collective-permute-start(f32[10,128,128]{2,1,0:T(8,128)S(1)} %slice.36), channel_id=1, source_target_pairs={{0,16},{4,20},{8,24},{12,28},{16,0},{20,4},{24,8},{28,12},{1,17},{... | collective-permute-start | bytes 1966088 | tf_op jit(solution)/shard_map/ppermute | solution.py:16
  64.8 14.8 %copy-start.8 = (f32[20,128,128]{2,1,0:T(8,128)}, f32[20,128,128]{2,1,0:T(8,128)S(1)}, u32[]{:S(2)}) copy-start(f32[20,128,128]{2,1,0:T(8,128)S(1)} %collective-permute-done.8.refs_9_) | copy-start | bytes 3932164
  64.8 14.8 %collective-permute-start.14 = (f32[10,128,128]{2,1,0:T(8,128)S(1)}, f32[10,128,128]{2,1,0:T(8,128)}, u32[]{:S(2)}, u32[]{:S(2)}) collective-permute-start(f32[10,128,128]{2,1,0:T(8,128)S(1)} %slice.37), channel_id=1, source_target_pairs={{0,8},{4,12},{8,0},{12,4},{16,24},{20,28},{24,16},{28,20},{1,9},{5... | collective-permute-start | bytes 1966088 | tf_op jit(solution)/shard_map/ppermute | solution.py:16
  66.3 38.0 %collective-permute-start.10 = (f32[20,128,128]{2,1,0:T(8,128)}, f32[20,128,128]{2,1,0:T(8,128)}, u32[]{:S(2)}, u32[]{:S(2)}) collective-permute-start(f32[20,128,128]{2,1,0:T(8,128)} %collective-permute-done.9.refs_10_), channel_id=1, source_target_pairs={{0,4},{4,0},{8,12},{12,8},{16,20},{20,16},{24,28},{28,24},{1,5},{5... | collective-permute-start | bytes 3932168 | tf_op jit(solution)/shard_map/ppermute | solution.py:16
  66.3 39.3 %collective-permute-start.12 = (f32[20,128,128]{2,1,0:T(8,128)}, f32[20,128,128]{2,1,0:T(8,128)}, u32[]{:S(2)}, u32[]{:S(2)}) collective-permute-start(f32[20,128,128]{2,1,0:T(8,128)} %collective-permute-done.11.refs_12_), channel_id=1, source_target_pairs={{0,4},{4,0},{8,12},{12,8},{16,20},{20,16},{24,28},{28,24},{1,5},{5... | collective-permute-start | bytes 3932168 | tf_op jit(solution)/shard_map/ppermute | solution.py:16
  78.2 23.3 %collective-permute-start.4 = (f32[12,128,128]{2,1,0:T(8,128)}, f32[12,128,128]{2,1,0:T(8,128)S(1)}, u32[]{:S(2)}, u32[]{:S(2)}) collective-permute-start(f32[12,128,128]{2,1,0:T(8,128)} %collective-permute-done.3.refs_7_), channel_id=1, source_target_pairs={{1,0},{2,1},{5,4},{6,5},{9,8},{10,9},{13,12},{14,13},{17,16},{18,1... | collective-permute-start | bytes 2359304 | tf_op jit(solution)/shard_map/ppermute | solution.py:16
  79.5 22.7 %collective-permute-start.15 = (f32[10,128,128]{2,1,0:T(8,128)}, f32[10,128,128]{2,1,0:T(8,128)}, u32[]{:S(2)}, u32[]{:S(2)}) collective-permute-start(f32[10,128,128]{2,1,0:T(8,128)} %collective-permute-done.13.refs_14_), channel_id=1, source_target_pairs={{0,4},{4,0},{8,12},{12,8},{16,20},{20,16},{24,28},{28,24},{1,5},{5... | collective-permute-start | bytes 1966088 | tf_op jit(solution)/shard_map/ppermute | solution.py:16
  79.6 23.9 %collective-permute-start.16 = (f32[10,128,128]{2,1,0:T(8,128)}, f32[10,128,128]{2,1,0:T(8,128)}, u32[]{:S(2)}, u32[]{:S(2)}) collective-permute-start(f32[10,128,128]{2,1,0:T(8,128)} %collective-permute-done.14.refs_15_), channel_id=1, source_target_pairs={{0,4},{4,0},{8,12},{12,8},{16,20},{20,16},{24,28},{28,24},{1,5},{5... | collective-permute-start | bytes 1966088 | tf_op jit(solution)/shard_map/ppermute | solution.py:16
  91.1 28.6 %copy-start.3 = (s32[512]{0:T(512)S(1)}, s32[512]{0:T(512)}, u32[]{:S(2)}) copy-start(s32[512]{0:T(512)} %select_n.143.refs_1_) | copy-start | bytes 6148
  101.5 28.2 %collective-permute-start.18 = (f32[12,128,128]{2,1,0:T(8,128)S(1)}, f32[12,128,128]{2,1,0:T(8,128)S(1)}, u32[]{:S(2)}, u32[]{:S(2)}) collective-permute-start(f32[12,128,128]{2,1,0:T(8,128)S(1)} %collective-permute-done.17.refs_2_), channel_id=1, source_target_pairs={{2,3},{6,7},{10,11},{14,15},{18,19},{22,23},{26,27},{30,31}} | collective-permute-start | bytes 2359304 | tf_op jit(solution)/shard_map/ppermute | solution.py:16
  102.2 27.5 %collective-permute-start.20 = (f32[12,128,128]{2,1,0:T(8,128)S(1)}, f32[12,128,128]{2,1,0:T(8,128)S(1)}, u32[]{:S(2)}, u32[]{:S(2)}) collective-permute-start(f32[12,128,128]{2,1,0:T(8,128)S(1)} %collective-permute-done.19.refs_3_), channel_id=1, source_target_pairs={{1,0},{5,4},{9,8},{13,12},{17,16},{21,20},{25,24},{29,28}} | collective-permute-start | bytes 2359304 | tf_op jit(solution)/shard_map/ppermute | solution.py:16
  103.5 29.5 %collective-permute-start.2 = (f32[12,128,128]{2,1,0:T(8,128)S(1)}, f32[12,128,128]{2,1,0:T(8,128)S(1)}, u32[]{:S(2)}, u32[]{:S(2)}) collective-permute-start(f32[12,128,128]{2,1,0:T(8,128)S(1)} %collective-permute-done.1.refs_4_), channel_id=1, source_target_pairs={{2,3},{6,7},{10,11},{14,15},{18,19},{22,23},{26,27},{30,31}} | collective-permute-start | bytes 2359304 | tf_op jit(solution)/shard_map/ppermute | solution.py:16
  104.2 36.1 %collective-permute-start.5 = (f32[12,128,128]{2,1,0:T(8,128)S(1)}, f32[12,128,128]{2,1,0:T(8,128)S(1)}, u32[]{:S(2)}, u32[]{:S(2)}) collective-permute-start(f32[12,128,128]{2,1,0:T(8,128)S(1)} %collective-permute-done.4.refs_5_), channel_id=1, source_target_pairs={{1,0},{5,4},{9,8},{13,12},{17,16},{21,20},{25,24},{29,28}} | collective-permute-start | bytes 2359304 | tf_op jit(solution)/shard_map/ppermute | solution.py:16
  119.7 4.0 %copy-start = (bf16[160,128,256]{2,1,0:T(8,128)(2,1)S(1)}, bf16[160,128,256]{2,1,0:T(8,128)(2,1)}, u32[]{:S(2)}) copy-start(bf16[160,128,256]{2,1,0:T(8,128)(2,1)} %get-tuple-element.7.refs_6_.refs_4_) | copy-start | bytes 31457284
  123.7 1.9 %copy-start.2 = (f32[48,128,128]{2,1,0:T(8,128)S(1)}, f32[48,128,128]{2,1,0:T(8,128)}, u32[]{:S(2)}) copy-start(f32[48,128,128]{2,1,0:T(8,128)} %get-tuple-element.8.refs_7_) | copy-start | bytes 9437188
  125.6 4.2 %copy-start.1 = (bf16[160,128,256]{2,1,0:T(8,128)(2,1)S(1)}, bf16[160,128,256]{2,1,0:T(8,128)(2,1)}, u32[]{:S(2)}) copy-start(bf16[160,128,256]{2,1,0:T(8,128)(2,1)} %get-tuple-element.7.refs_6_.refs_4_) | copy-start | bytes 31457284

commit v2 on v0

v2 whole, which is shorter than its diff:
```python
import functools

import jax
import jax.numpy as jnp
from jax import lax
from jax.experimental import pallas as pl
from jax.experimental.pallas import tpu as pltpu
from jax.sharding import PartitionSpec as P

SC = 48
GROUP = 32
F32, BF16 = jnp.float32, jnp.bfloat16
ANY = pl.BlockSpec(memory_space=pl.ANY)
SMEM = pl.BlockSpec(memory_space=pltpu.SMEM)
VMEM = pl.BlockSpec(memory_space=pltpu.VMEM)
SHORT = pl.CostEstimate(flops=1 << 16, bytes_accessed=1 << 16, transcendentals=0)


def together(*values):
    return lax.optimization_barrier(values)


def in_hbm(x):
    return pltpu.with_memory_space_constraint(x, pltpu.HBM)


def in_vmem(x):
    return pltpu.with_memory_space_constraint(x, pltpu.VMEM)


def rest_of_rows(held, half, rows, swap):
    halves = {code: (parts[0][:half], parts[0][half:]) for code, parts in held.items()}
    for code in range(2, rows, 2):
        if code not in held:
            low, high = code & -code, 1 << (code.bit_length() - 1)
            halves[code] = (swap(halves[code ^ high][0], high), swap(halves[code ^ low][1], low))
            held[code] = list(halves[code])


def split(x):
    high = x.astype(BF16)
    return high, (x - high.astype(F32)).astype(BF16)


def product(left, right):
    both = jnp.dot(left, jnp.concatenate([right, right], 0), preferred_element_type=F32)
    n = both.shape[1] // 2
    return both[:, :n] + both[:, n:]


def split_into(source, target):
    n = source.shape[-1]

    @pl.loop(0, source.shape[0])
    def _(i):
        high, low = split(source[i])
        target[i, :, :n] = high
        target[i, :, n:] = low


def panel_at(info, cols, per_device, step, q):
    col = info[1]
    holder = col + step * (1 - 2 * (col & 1))
    valid = (holder >= 0) & (holder < cols)
    panel = jnp.where(valid, holder * per_device + q, 0)
    return panel, jnp.where(valid, info[2 + panel], 0)


def add_list(info, lists_at, per_list, panel, count, a_split, b_split, acc):
    @pl.loop(0, (count + GROUP - 1) // GROUP)
    def _(g):
        terms, slots = [], []
        for u in range(GROUP):
            entry = info[lists_at + panel * per_list + g * GROUP + u]
            slots.append(entry & 1023)
            terms.append(product(a_split[entry >> 20], b_split[(entry >> 10) & 1023]))
        for slot, term in zip(slots, terms):
            acc[slot] += term


def panel_kernel(sizes, per_list, steps, ahead, pieces, first, info, *refs):
    cols, rows, per_device = sizes
    sources = 1 + max(step[0] for step in steps)
    a_refs, b_refs = refs[:sources], refs[sources : sources + len(pieces)]
    acc, *refs = refs[sources + len(pieces) + (not first) :]
    readies, refs = refs[: len(ahead)], refs[len(ahead) :]
    a_buf, b_buf, a_split, b_split, a_sem, b_sem = refs
    row, lists_at = info[0], 2 + rows

    def fetch(t, panel, count):
        for (code, at), b_ref in zip(pieces, b_refs):

            @pl.when((count > 0) & (code == (panel ^ row)))
            def _():
                pltpu.make_async_copy(b_ref, b_buf.at[t, pl.ds(at, b_ref.shape[0])], b_sem.at[t]).start()

    def fetched(t):
        return pltpu.make_async_copy(b_buf.at[t], b_buf.at[t], b_sem.at[t])

    found = [panel_at(info, cols, per_device, step, q) for _, _, step, q in steps]
    found += [panel_at(info, cols, per_device, step, q) for step, q in ahead]
    for t, (panel, count) in enumerate(found):
        fetch(t, panel, count)
        if t < len(steps):
            a_ref = a_refs[steps[t][0]].at[steps[t][1]]

            @pl.when(count > 0)
            def _():
                pltpu.make_async_copy(a_ref, a_buf.at[t], a_sem.at[t]).start()

    if first:
        acc[...] = jnp.zeros_like(acc)
    for t in range(len(steps)):
        panel, count = found[t]
        a_ref = a_refs[steps[t][0]].at[steps[t][1]]

        @pl.when(count > 0)
        def _():
            pltpu.make_async_copy(a_ref, a_buf.at[t], a_sem.at[t]).wait()
            split_into(a_buf.at[t], a_split)
            fetched(t).wait()
            split_into(b_buf.at[t], b_split)

        add_list(info, lists_at, per_list, panel, count, a_split, b_split, acc)
    for j, ready in enumerate(readies):
        t = len(steps) + j

        @pl.when(found[t][1] > 0)
        def _():
            fetched(t).wait()
            split_into(b_buf.at[t], ready)


def ready_kernel(sizes, per_list, step, q, last, info, a_ref, b_split, _, acc, *refs):
    if last:
        out, *refs = refs
    a_split, out_sem = refs
    panel, count = panel_at(info, sizes[0], sizes[2], step, q)

    @pl.when(count > 0)
    def _():
        split_into(a_ref, a_split)

    add_list(info, 2 + sizes[1], per_list, panel, count, a_split, b_split, acc)
    if last:
        done = pltpu.make_async_copy(acc.at[pl.ds(0, SC)], out, out_sem)
        done.start()
        done.wait()


def add_panels(sizes, per_list, info, items, b_held, acc, ahead):
    _, a_slots, size, _ = items[0][0].shape
    steps = tuple((i, j, step, q + j) for i, (a, step, q) in enumerate(items) for j in range(a.shape[0]))
    a_list = [in_hbm(a) for a, _, _ in items]
    b_slots = sum(piece.shape[0] for piece in b_held[0])
    pieces, b_list = [], []
    for code, parts in enumerate(b_held):
        offset = 0
        for part in parts:
            pieces.append((code, offset))
            b_list.append(in_hbm(part))
            offset += part.shape[0]
    count = len(steps) + len(ahead)
    ready = jax.ShapeDtypeStruct((b_slots, size, 2 * size), BF16)
    first = acc is None
    return pl.pallas_call(
        functools.partial(panel_kernel, sizes, per_list, steps, tuple(ahead), tuple(pieces), first),
        out_shape=[jax.ShapeDtypeStruct((SC + 1, size, size), F32)] + [ready] * len(ahead),
        in_specs=[SMEM] + [ANY] * (len(a_list) + len(b_list)) + ([] if first else [VMEM]),
        out_specs=[VMEM] * (1 + len(ahead)),
        input_output_aliases={} if first else {1 + len(a_list) + len(b_list): 0},
        scratch_shapes=[
            pltpu.VMEM((len(steps), a_slots, size, size), F32),
            pltpu.VMEM((count, b_slots, size, size), F32),
            pltpu.VMEM((a_slots, size, 2 * size), BF16),
            pltpu.VMEM((b_slots, size, 2 * size), BF16),
            pltpu.SemaphoreType.DMA((len(steps),)),
            pltpu.SemaphoreType.DMA((count,)),
        ],
        compiler_params=pltpu.CompilerParams(vmem_limit_bytes=24 << 20),
        cost_estimate=SHORT,
        name="add_panels",
    )(info, *a_list, *b_list, *([] if first else [acc]))


def add_ready(sizes, per_list, info, a, step, q, b_ready, acc, last):
    a_slots, size, _ = a.shape
    out = [jax.ShapeDtypeStruct(acc.shape, F32)]
    if last:
        out.append(jax.ShapeDtypeStruct((SC, size, size), F32))
    return pl.pallas_call(
        functools.partial(ready_kernel, sizes, per_list, step, q, last),
        out_shape=out,
        in_specs=[SMEM, VMEM, VMEM, VMEM],
        out_specs=[VMEM, ANY][: len(out)],
        input_output_aliases={3: 0},
        scratch_shapes=[pltpu.VMEM((a_slots, size, 2 * size), BF16), pltpu.SemaphoreType.DMA],
        compiler_params=pltpu.CompilerParams(vmem_limit_bytes=16 << 20),
        cost_estimate=SHORT,
        name="add_last",
    )(info, in_vmem(a), b_ready, acc)[-1]


def on_device(cols, rows, a_blocks, b_blocks, product_lists):
    own, b_own = a_blocks[0], b_blocks[0, 0]
    per_device = own.shape[0]
    sizes = (cols, rows, per_device)
    entries = product_lists[0, 0]
    per_list = -(-entries.shape[1] // GROUP) * GROUP
    entries = jnp.pad(entries, ((0, 0), (0, per_list - entries.shape[1]), (0, 0)), constant_values=SC)
    real = entries[:, :, 2] < SC
    packed = jnp.where(real, (entries[:, :, 0] << 20) | (entries[:, :, 1] << 10) | entries[:, :, 2], SC)
    counts = jnp.sum(real.astype(jnp.int32), axis=1)
    place = jnp.stack([lax.axis_index("row"), lax.axis_index("col")]).astype(jnp.int32)
    info = jnp.concatenate([place, counts, packed.reshape(-1)])

    def over_even(value):
        return lax.ppermute(value, "col", [(i, i ^ 1) for i in range(cols) if i ^ 1 < cols])

    def over_odd(value):
        return lax.ppermute(value, "col", [(i, j) for i in range(cols) for j in [((i + 1) ^ 1) - 1] if 0 <= j < cols])

    def swap(value, bit):
        return lax.ppermute(value, "row", [(i, i ^ bit) for i in range(rows)])

    half = b_own.shape[0] // 2
    bits = [1 << i for i in range(1, rows.bit_length()) if (1 << i) < rows]
    x, y = over_even(own), over_odd(own)
    b_held = {0: [b_own]}
    b_held.update({bit: [swap(b_own, bit)] for bit in bits})
    stages = [[(own, 0, 0), (x, 1, 0), (y, -1, 0)]]

    even, odd = [x[q] for q in range(per_device)], y
    for s in range(2, cols):
        hop, other = (over_odd, over_even) if s % 2 == 0 else (over_even, over_odd)
        even = [hop(piece) for piece in even]
        if s < cols - 1:
            odd = other(odd)
            near_even = 1 if s % 2 else -1
            stages.append([(piece[None], near_even * s, q) for q, piece in enumerate(even)] + [(odd, -near_even * s, 0)])
        if s == 2:
            even[0], near = together(even[0], [b_held[bit] for bit in bits])
            b_held.update(zip(bits, near))
            rest_of_rows(b_held, half, rows, swap)
        if s == 3:
            stages[0][0] = (together(own, stages[1][-1][0])[0], 0, 0)
    b_held.update({code | 1: [swap(piece, 1) for piece in b_held[code]] for code in range(0, rows, 2)})
    b_held = [b_held[code] for code in range(rows)]
    acc, readies = None, []
    for i, items in enumerate(stages):
        ahead = [(cols - 1, q) for q in range(per_device)] if i == len(stages) - 1 else []
        acc, *readies = add_panels(sizes, per_list, info, items, b_held, acc, ahead)
    for q, piece in enumerate(even):
        acc = add_ready(sizes, per_list, info, piece, cols - 1, q, readies[q], acc, q == per_device - 1)
    return acc.reshape((1, 1) + acc.shape)


def solution(mesh):
    spec = P("row", "col", None, None, None)
    return jax.shard_map(
        functools.partial(on_device, mesh.shape["col"], mesh.shape["row"]),
        mesh=mesh,
        in_specs=(spec, spec, spec),
        out_specs=spec,
        check_vma=False,
    )
```

time: 559 us -> 117 us (0.21)
  waiting for transfers between devices: 351 us -> 56.7 us
  matrix products: 105 us -> 0 us
  local copies, waits for them, and re-layouts: 71.5 us -> 3.36 us
  starting transfers between devices: 0.04 us -> 32.7 us
  Pallas kernels: 0 us -> 23.5 us
  other arithmetic: 16.7 us -> 0.2 us
  between operations: 13.4 us -> 0.14 us
    psum x8 -> x0, waiting for transfers between devices: 351 us -> none  [spread(): return lax.psum(block, axis)]
    dot_general x16 -> x0, matrix products: 105 us -> none  [the longest x8 57.7 us: apply_panel(): jnp.einsum('pij,pjk->pik', left_sel, right_sel, precision=lax.Precision.H...]
    ppermute x7 -> x16, waiting for transfers between devices: 0.02 us -> 56.7 us  [the longest x4 40 us: over_even(): lax.ppermute(value, 'col', [(i, i ^ 1) for i in range(cols) if i ^ 1 < co...]
    gather x16 -> x0, local copies, waits for them, and re-layouts: 53.5 us -> none  [the longest x8 31.2 us: apply_panel(): left_sel = jnp.take(left, entries[:, 0], axis=0)]
    ppermute x7 -> x16, starting transfers between devices: 0.02 us -> 32.7 us  [the longest x4 21.9 us: over_even(): lax.ppermute(value, 'col', [(i, i ^ 1) for i in range(cols) if i ^ 1 < co...]
    pallas_call x0 -> x4, Pallas kernels: none -> 23.5 us  [the longest x2 17.9 us: add_panels(): pl.pallas_call(functools.partial(panel_kernel, sizes, per_list, steps, tu...]
    select_n x8 -> x1, other arithmetic: 16.6 us -> 0.01 us  [on_device(): jnp.where(real, entries[:, :, 0] << 20 | entries[:, :, 1] << 10 | entries...]
    while x36 -> x0, local copies, waits for them, and re-layouts: 16.6 us -> none
  transfers between devices with their start and end apart: 15 -> 16, of which waited for: 8 -> 6; matrix products, arithmetic and copies ran while one was open for 8% -> 1% of each run, Pallas kernels for 0% -> 17%
where the time goes in v2:
time: 117 us
  waiting for transfers between devices  56.7 us (48%)
  starting transfers between devices  32.7 us (28%)
  Pallas kernels  23.5 us (20%)
  local copies, waits for them, and re-layouts  3.36 us (3%)
    ppermute x4, waiting for transfers between devices, over_even(): lax.ppermute(value, 'col', [(i, i ^ 1) for i in range(cols) if i ^ 1 < co...  40 us
    ppermute x4, starting transfers between devices, over_even(): lax.ppermute(value, 'col', [(i, i ^ 1) for i in range(cols) if i ^ 1 < co...  21.9 us
    pallas_call x2, Pallas kernels, add_panels(): pl.pallas_call(functools.partial(panel_kernel, sizes, per_list, steps, tu...  17.9 us
    ppermute x9, waiting for transfers between devices, swap(): return lax.ppermute(value, 'row', [(i, i ^ bit) for i in range(rows)])  16.7 us
    ppermute x9, starting transfers between devices, swap(): return lax.ppermute(value, 'row', [(i, i ^ bit) for i in range(rows)])  6.8 us
    pallas_call x2, Pallas kernels, add_ready(): pl.pallas_call(functools.partial(ready_kernel, sizes, per_list, step, q,...  5.55 us
    ppermute x3, starting transfers between devices, over_odd(): lax.ppermute(value, 'col', [(i, j) for i in range(cols) for j in [(i + 1...  4 us
  transfers between devices with their start and end apart: 16, of which 6 were waited for; matrix products, arithmetic and copies ran while one was open for 1% of the time, Pallas kernels for 17%

profile of v2, /device:TPU:0, one launch (start us, length us, event | category | flops | bytes accessed | tf_op | source)
XLA Modules:
  0.0 116.5 jit_solution(8315190317822707277)
XLA Ops:
  0.0 3.0 %collective-permute-start = (f32[2,12,128,128]{3,2,1,0:T(8,128)}, f32[2,12,128,128]{3,2,1,0:T(8,128)S(1)}, u32[]{:S(2)}, u32[]{:S(2)}) collective-permute-start(f32[2,12,128,128]{3,2,1,0:T(8,128)} %bitcast.19), channel_id=1, source_target_pairs={{0,1},{1,0},{2,3},{3,2},{4,5},{5,4},{6,7},{7,6},{8,9},{9,8},{10,11... | collective-permute-start | bytes 4718600 | tf_op jit(solution)/shard_map/ppermute | solution.py:218
  3.0 0.7 collective-permute-start.4
  3.8 0.0 copy-start.2
  3.8 1.6 %collective-permute-start.7 = (f32[20,128,128]{2,1,0:T(8,128)}, f32[20,128,128]{2,1,0:T(8,128)S(1)}, u32[]{:S(2)}, u32[]{:S(2)}) collective-permute-start(f32[20,128,128]{2,1,0:T(8,128)} %bitcast.14), channel_id=1, source_target_pairs={{0,8},{4,12},{8,0},{12,4},{16,24},{20,28},{24,16},{28,20},{1,9},{5... | collective-permute-start | bytes 3932168 | tf_op jit(solution)/shard_map/ppermute | solution.py:224
  5.4 1.5 %collective-permute-start.8 = (f32[20,128,128]{2,1,0:T(8,128)}, f32[20,128,128]{2,1,0:T(8,128)}, u32[]{:S(2)}, u32[]{:S(2)}) collective-permute-start(f32[20,128,128]{2,1,0:T(8,128)} %bitcast.15), channel_id=1, source_target_pairs={{0,16},{4,20},{8,24},{12,28},{16,0},{20,4},{24,8},{28,12},{1,17},{... | collective-permute-start | bytes 3932168 | tf_op jit(solution)/shard_map/ppermute | solution.py:224
  6.9 30.8 %collective-permute-done.refs_1_ = f32[2,12,128,128]{3,2,1,0:T(8,128)S(1)} collective-permute-done((f32[2,12,128,128]{3,2,1,0:T(8,128)}, f32[2,12,128,128]{3,2,1,0:T(8,128)S(1)}, u32[]{:S(2)}, u32[]{:S(2)}) %collective-permute-start) | collective-permute-done | bytes 1572896 | tf_op jit(solution)/shard_map/ppermute | solution.py:218
  37.6 0.1 slice_bitcast_fusion
  37.8 1.0 copy-done.1
  38.8 1.7 %collective-permute-start.3 = (f32[12,128,128]{2,1,0:T(8,128)S(1)}, f32[12,128,128]{2,1,0:T(8,128)}, u32[]{:S(2)}, u32[]{:S(2)}) collective-permute-start(f32[12,128,128]{2,1,0:T(8,128)S(1)} %get-tuple-element.23), channel_id=1, source_target_pairs={{1,2},{2,1},{5,6},{6,5},{9,10},{10,9},{13,14},{14,13},{17,18},{18,... | collective-permute-start | bytes 2359304 | tf_op jit(solution)/shard_map/ppermute | solution.py:221
  40.5 0.0 copy-done.2
  40.5 0.0 collective-permute-start.6
  40.5 0.0 collective-permute-done.4.refs_2_
  40.5 0.0 copy-start.6
  40.5 3.8 %collective-permute-start.5 = (f32[2,12,128,128]{3,2,1,0:T(8,128)S(1)}, f32[2,12,128,128]{3,2,1,0:T(8,128)S(1)}, u32[]{:S(2)}, u32[]{:S(2)}) collective-permute-start(f32[2,12,128,128]{3,2,1,0:T(8,128)S(1)} %collective-permute-done.4.refs_2_), channel_id=1, source_target_pairs={{0,1},{1,0},{2,3},{3,2},{4,5},{5,4},{6,7},{7,6},{8,9},{9,8},{10,11... | collective-permute-start | bytes 4718600 | tf_op jit(solution)/shard_map/ppermute | solution.py:218
  44.3 0.0 collective-permute-done.7.refs_5_
  44.3 1.6 %collective-permute-start.1 = (f32[12,128,128]{2,1,0:T(8,128)S(1)}, f32[12,128,128]{2,1,0:T(8,128)}, u32[]{:S(2)}, u32[]{:S(2)}) collective-permute-start(f32[12,128,128]{2,1,0:T(8,128)S(1)} %get-tuple-element.24), channel_id=1, source_target_pairs={{1,2},{2,1},{5,6},{6,5},{9,10},{10,9},{13,14},{14,13},{17,18},{18,... | collective-permute-start | bytes 2359304 | tf_op jit(solution)/shard_map/ppermute | solution.py:221
  45.9 0.0 collective-permute-done.8.refs_7_
  45.9 0.0 collective-permute-done.3
  46.0 1.6 %collective-permute-start.11 = (f32[10,128,128]{2,1,0:T(8,128)S(1)}, f32[10,128,128]{2,1,0:T(8,128)S(1)}, u32[]{:S(2)}, u32[]{:S(2)}) collective-permute-start(f32[10,128,128]{2,1,0:T(8,128)S(1)} %slice.27), channel_id=1, source_target_pairs={{0,16},{4,20},{8,24},{12,28},{16,0},{20,4},{24,8},{28,12},{1,17},{... | collective-permute-start | bytes 1966088 | tf_op jit(solution)/shard_map/ppermute | solution.py:224
  47.5 1.1 slice.28
  48.7 1.6 %collective-permute-start.12 = (f32[10,128,128]{2,1,0:T(8,128)S(1)}, f32[10,128,128]{2,1,0:T(8,128)}, u32[]{:S(2)}, u32[]{:S(2)}) collective-permute-start(f32[10,128,128]{2,1,0:T(8,128)S(1)} %slice.28), channel_id=1, source_target_pairs={{0,8},{4,12},{8,0},{12,4},{16,24},{20,28},{24,16},{28,20},{1,9},{5... | collective-permute-start | bytes 1966088 | tf_op jit(solution)/shard_map/ppermute | solution.py:224
  50.2 12.6 %collective-permute-done.11.refs_9_ = f32[10,128,128]{2,1,0:T(8,128)S(1)} collective-permute-done((f32[10,128,128]{2,1,0:T(8,128)S(1)}, f32[10,128,128]{2,1,0:T(8,128)S(1)}, u32[]{:S(2)}, u32[]{:S(2)}) %collective-permute-start.11) | collective-permute-done | bytes 655392 | tf_op jit(solution)/shard_map/ppermute | solution.py:224
  62.8 0.0 collective-permute-start.13
  62.8 0.0 collective-permute-done.6.refs_4_
  62.8 0.0 copy-start.3
  62.8 0.5 collective-permute-start.10
  63.3 0.0 collective-permute-done.1
  63.3 0.1 collective-permute-start.9
  63.4 1.9 %collective-permute-done.12.refs_10_ = f32[10,128,128]{2,1,0:T(8,128)} collective-permute-done((f32[10,128,128]{2,1,0:T(8,128)S(1)}, f32[10,128,128]{2,1,0:T(8,128)}, u32[]{:S(2)}, u32[]{:S(2)}) %collective-permute-start.12) | collective-permute-done | bytes 655392 | tf_op jit(solution)/shard_map/ppermute | solution.py:224
  65.4 13.3 %collective-permute-start.15 = (f32[12,128,128]{2,1,0:T(8,128)}, f32[12,128,128]{2,1,0:T(8,128)S(1)}, u32[]{:S(2)}, u32[]{:S(2)}) collective-permute-start(f32[12,128,128]{2,1,0:T(8,128)} %collective-permute-done.3), channel_id=1, source_target_pairs={{0,1},{1,0},{2,3},{3,2},{4,5},{5,4},{6,7},{7,6},{8,9},{9,8},{10,11... | collective-permute-start | bytes 2359304 | tf_op jit(solution)/shard_map/ppermute | solution.py:218
  78.6 0.7 collective-permute-done.5.refs_2_
  79.3 1.8 %collective-permute-start.2 = (f32[12,128,128]{2,1,0:T(8,128)}, f32[12,128,128]{2,1,0:T(8,128)S(1)}, u32[]{:S(2)}, u32[]{:S(2)}) collective-permute-start(f32[12,128,128]{2,1,0:T(8,128)} %collective-permute-done.1), channel_id=1, source_target_pairs={{0,1},{1,0},{2,3},{3,2},{4,5},{5,4},{6,7},{7,6},{8,9},{9,8},{10,11... | collective-permute-start | bytes 2359304 | tf_op jit(solution)/shard_map/ppermute | solution.py:218
  81.1 0.0 collective-permute-done.13.refs_11_
  81.1 0.9 copy-done.5
  82.0 0.0 collective-permute-start.14
  82.0 0.0 copy-done.6
  82.0 0.1 convert_reduce_fusion
  82.1 0.1 select_n.9
  82.2 0.1 pad_add_fusion.info
  82.3 2.1 %collective-permute-done.14.refs_12_ = f32[10,128,128]{2,1,0:T(8,128)} collective-permute-done((f32[10,128,128]{2,1,0:T(8,128)}, f32[10,128,128]{2,1,0:T(8,128)}, u32[]{:S(2)}, u32[]{:S(2)}) %collective-permute-start.14) | collective-permute-done | bytes 655392 | tf_op jit(solution)/shard_map/ppermute | solution.py:224
  84.4 0.0 collective-permute-done.10.refs_8_
  84.4 0.0 collective-permute-done.9.refs_6_
  84.4 10.7 %add_panels.2.refs_13_ = f32[49,128,128]{2,1,0:T(8,128)S(1)} custom-call(s32[522]{0:T(1024)S(1)} %pad_add_fusion.info, f32[2,12,128,128]{3,2,1,0:T(8,128)} %bitcast.21, f32[2,12,128,128]{3,2,1,0:T(8,128)} %copy-done.1, f32[2,12,128,128]{3,2,1,0:T(8,128)} %copy-done.6, f32[20,128,128]{2,1,0:T(8,128)} %bitcast.16, f32[20,128,128]{2,1,0:T(8,128)} %copy-done.3, ...), custom_call_target="tpu_custom_call" | custom-call | flops 65536 | bytes 65536 | tf_op jit(solution)/shard_map/add_panels/pallas_call | solution.py:166
  95.1 7.2 %add_panels.3 = (f32[49,128,128]{2,1,0:T(8,128)S(1)}, bf16[20,128,256]{2,1,0:T(8,128)(2,1)S(1)}, bf16[20,128,256]{2,1,0:T(8,128)(2,1)S(1)}) custom-call(s32[522]{0:T(1024)S(1)} %pad_add_fusion.info, f32[1,12,128,128]{3,2,1,0:T(8,128)} %bitcast.6.refs_0_, f32[1,12,128,128]{3,2,1,0:T(8,128)} %bitcast.7.refs_1_, ...), custom_call_target="tpu_custom_call", output_to_operand_aliasing={{0}: (14, {})} | custom-call | flops 65536 | bytes 65536 | tf_op jit(solution)/shard_map/add_panels/pallas_call | solution.py:166
  102.4 0.0 collective-permute-done.15.a_ref
  102.4 2.3 %add_last.2._ = f32[49,128,128]{2,1,0:T(8,128)S(1)} custom-call(s32[522]{0:T(1024)S(1)} %pad_add_fusion.info, f32[12,128,128]{2,1,0:T(8,128)S(1)} %collective-permute-done.15.a_ref, bf16[20,128,256]{2,1,0:T(8,128)(2,1)S(1)} %get-tuple-element.18.b_split, f32[49,128,128]{2,1,0:T(8,128)S(1)} %get-tuple-element.19._), custom_call_target="tpu_custom_call", output_to_operand_aliasing={{}: (3, {})} | custom-call | flops 65536 | bytes 65536 | tf_op jit(solution)/shard_map/add_last/pallas_call | solution.py:191
  104.7 8.6 %collective-permute-done.2.a_ref = f32[12,128,128]{2,1,0:T(8,128)S(1)} collective-permute-done((f32[12,128,128]{2,1,0:T(8,128)}, f32[12,128,128]{2,1,0:T(8,128)S(1)}, u32[]{:S(2)}, u32[]{:S(2)}) %collective-permute-start.2) | collective-permute-done | bytes 786464 | tf_op jit(solution)/shard_map/ppermute | solution.py:218
  113.3 3.2 %add_last.3 = (f32[49,128,128]{2,1,0:T(8,128)S(1)}, f32[48,128,128]{2,1,0:T(8,128)}) custom-call(s32[522]{0:T(1024)S(1)} %pad_add_fusion.info, f32[12,128,128]{2,1,0:T(8,128)S(1)} %collective-permute-done.2.a_ref, bf16[20,128,256]{2,1,0:T(8,128)(2,1)S(1)} %get-tuple-element.16.b_split, f32[49,128,128]{2,1,0:T(8,128)S(1)} %add_last.2._), custom_call_target="tpu_custom_call", output_to_operand_aliasing={{0}: (3, {})} | custom-call | flops 65536 | bytes 65536 | tf_op jit(solution)/shard_map/add_last/pallas_call | solution.py:191
  (13 shorter events, 0.1 us)
Async XLA Ops:
  0.0 37.6 %collective-permute-start = (f32[2,12,128,128]{3,2,1,0:T(8,128)}, f32[2,12,128,128]{3,2,1,0:T(8,128)S(1)}, u32[]{:S(2)}, u32[]{:S(2)}) collective-permute-start(f32[2,12,128,128]{3,2,1,0:T(8,128)} %bitcast.19), channel_id=1, source_target_pairs={{0,1},{1,0},{2,3},{3,2},{4,5},{5,4},{6,7},{7,6},{8,9},{9,8},{10,11... | collective-permute-start | bytes 4718600 | tf_op jit(solution)/shard_map/ppermute | solution.py:218
  3.0 37.5 %collective-permute-start.4 = (f32[2,12,128,128]{3,2,1,0:T(8,128)}, f32[2,12,128,128]{3,2,1,0:T(8,128)S(1)}, u32[]{:S(2)}, u32[]{:S(2)}) collective-permute-start(f32[2,12,128,128]{3,2,1,0:T(8,128)} %bitcast.20), channel_id=1, source_target_pairs={{1,2},{2,1},{5,6},{6,5},{9,10},{10,9},{13,14},{14,13},{17,18},{18,... | collective-permute-start | bytes 4718600 | tf_op jit(solution)/shard_map/ppermute | solution.py:221
  3.8 36.7 %copy-start.2 = (f32[1,1,20,128,128]{4,3,2,1,0:T(8,128)S(1)}, f32[1,1,20,128,128]{4,3,2,1,0:T(8,128)}, u32[]{:S(2)}) copy-start(f32[1,1,20,128,128]{4,3,2,1,0:T(8,128)} %param.4) | copy-start | bytes 3932164
  3.8 40.6 %collective-permute-start.7 = (f32[20,128,128]{2,1,0:T(8,128)}, f32[20,128,128]{2,1,0:T(8,128)S(1)}, u32[]{:S(2)}, u32[]{:S(2)}) collective-permute-start(f32[20,128,128]{2,1,0:T(8,128)} %bitcast.14), channel_id=1, source_target_pairs={{0,8},{4,12},{8,0},{12,4},{16,24},{20,28},{24,16},{28,20},{1,9},{5... | collective-permute-start | bytes 3932168 | tf_op jit(solution)/shard_map/ppermute | solution.py:224
  5.4 40.6 %collective-permute-start.8 = (f32[20,128,128]{2,1,0:T(8,128)}, f32[20,128,128]{2,1,0:T(8,128)}, u32[]{:S(2)}, u32[]{:S(2)}) collective-permute-start(f32[20,128,128]{2,1,0:T(8,128)} %bitcast.15), channel_id=1, source_target_pairs={{0,16},{4,20},{8,24},{12,28},{16,0},{20,4},{24,8},{28,12},{1,17},{... | collective-permute-start | bytes 3932168 | tf_op jit(solution)/shard_map/ppermute | solution.py:224
  37.6 1.2 %copy-start.1 = (f32[2,12,128,128]{3,2,1,0:T(8,128)}, f32[2,12,128,128]{3,2,1,0:T(8,128)S(1)}, u32[]{:S(2)}) copy-start(f32[2,12,128,128]{3,2,1,0:T(8,128)S(1)} %collective-permute-done.refs_1_) | copy-start | bytes 4718596
  38.8 43.2 %copy-start.8 = (s32[1,1,8,64,3]{3,2,4,1,0:T(8,128)S(1)}, s32[1,1,8,64,3]{3,2,4,1,0:T(8,128)}, u32[]{:S(2)}) copy-start(s32[1,1,8,64,3]{3,2,4,1,0:T(8,128)} %param.5) | copy-start | bytes 18436
  38.8 7.1 %collective-permute-start.3 = (f32[12,128,128]{2,1,0:T(8,128)S(1)}, f32[12,128,128]{2,1,0:T(8,128)}, u32[]{:S(2)}, u32[]{:S(2)}) collective-permute-start(f32[12,128,128]{2,1,0:T(8,128)S(1)} %get-tuple-element.23), channel_id=1, source_target_pairs={{1,2},{2,1},{5,6},{6,5},{9,10},{10,9},{13,14},{14,13},{17,18},{18,... | collective-permute-start | bytes 2359304 | tf_op jit(solution)/shard_map/ppermute | solution.py:221
  40.5 22.3 %collective-permute-start.6 = (f32[20,128,128]{2,1,0:T(8,128)S(1)}, f32[20,128,128]{2,1,0:T(8,128)S(1)}, u32[]{:S(2)}, u32[]{:S(2)}) collective-permute-start(f32[20,128,128]{2,1,0:T(8,128)S(1)} %bitcast.18), channel_id=1, source_target_pairs={{0,4},{4,0},{8,12},{12,8},{16,20},{20,16},{24,28},{28,24},{1,5},{5... | collective-permute-start | bytes 3932168 | tf_op jit(solution)/shard_map/ppermute | solution.py:224
  40.5 41.5 %copy-start.6 = (f32[2,12,128,128]{3,2,1,0:T(8,128)}, f32[2,12,128,128]{3,2,1,0:T(8,128)S(1)}, u32[]{:S(2)}) copy-start(f32[2,12,128,128]{3,2,1,0:T(8,128)S(1)} %collective-permute-done.4.refs_2_) | copy-start | bytes 4718596
  40.5 38.8 %collective-permute-start.5 = (f32[2,12,128,128]{3,2,1,0:T(8,128)S(1)}, f32[2,12,128,128]{3,2,1,0:T(8,128)S(1)}, u32[]{:S(2)}, u32[]{:S(2)}) collective-permute-start(f32[2,12,128,128]{3,2,1,0:T(8,128)S(1)} %collective-permute-done.4.refs_2_), channel_id=1, source_target_pairs={{0,1},{1,0},{2,3},{3,2},{4,5},{5,4},{6,7},{7,6},{8,9},{9,8},{10,11... | collective-permute-start | bytes 4718600 | tf_op jit(solution)/shard_map/ppermute | solution.py:218
  44.3 40.1 %copy-start = (f32[20,128,128]{2,1,0:T(8,128)}, f32[20,128,128]{2,1,0:T(8,128)S(1)}, u32[]{:S(2)}) copy-start(f32[20,128,128]{2,1,0:T(8,128)S(1)} %collective-permute-done.7.refs_5_) | copy-start | bytes 3932164
  44.3 19.0 %collective-permute-start.1 = (f32[12,128,128]{2,1,0:T(8,128)S(1)}, f32[12,128,128]{2,1,0:T(8,128)}, u32[]{:S(2)}, u32[]{:S(2)}) collective-permute-start(f32[12,128,128]{2,1,0:T(8,128)S(1)} %get-tuple-element.24), channel_id=1, source_target_pairs={{1,2},{2,1},{5,6},{6,5},{9,10},{10,9},{13,14},{14,13},{17,18},{18,... | collective-permute-start | bytes 2359304 | tf_op jit(solution)/shard_map/ppermute | solution.py:221
  46.0 16.9 %collective-permute-start.11 = (f32[10,128,128]{2,1,0:T(8,128)S(1)}, f32[10,128,128]{2,1,0:T(8,128)S(1)}, u32[]{:S(2)}, u32[]{:S(2)}) collective-permute-start(f32[10,128,128]{2,1,0:T(8,128)S(1)} %slice.27), channel_id=1, source_target_pairs={{0,16},{4,20},{8,24},{12,28},{16,0},{20,4},{24,8},{28,12},{1,17},{... | collective-permute-start | bytes 1966088 | tf_op jit(solution)/shard_map/ppermute | solution.py:224
  48.7 16.7 %collective-permute-start.12 = (f32[10,128,128]{2,1,0:T(8,128)S(1)}, f32[10,128,128]{2,1,0:T(8,128)}, u32[]{:S(2)}, u32[]{:S(2)}) collective-permute-start(f32[10,128,128]{2,1,0:T(8,128)S(1)} %slice.28), channel_id=1, source_target_pairs={{0,8},{4,12},{8,0},{12,4},{16,24},{20,28},{24,16},{28,20},{1,9},{5... | collective-permute-start | bytes 1966088 | tf_op jit(solution)/shard_map/ppermute | solution.py:224
  62.8 21.6 %copy-start.4 = (f32[10,128,128]{2,1,0:T(8,128)}, f32[10,128,128]{2,1,0:T(8,128)S(1)}, u32[]{:S(2)}) copy-start(f32[10,128,128]{2,1,0:T(8,128)S(1)} %collective-permute-done.11.refs_9_) | copy-start | bytes 1966084
  62.8 18.3 %collective-permute-start.13 = (f32[10,128,128]{2,1,0:T(8,128)S(1)}, f32[10,128,128]{2,1,0:T(8,128)S(1)}, u32[]{:S(2)}, u32[]{:S(2)}) collective-permute-start(f32[10,128,128]{2,1,0:T(8,128)S(1)} %collective-permute-done.11.refs_9_), channel_id=1, source_target_pairs={{0,4},{4,0},{8,12},{12,8},{16,20},{20,16},{24,28},{28,24},{1,5},{5... | collective-permute-start | bytes 1966088 | tf_op jit(solution)/shard_map/ppermute | solution.py:224
  62.8 15.8 %copy-start.3 = (f32[20,128,128]{2,1,0:T(8,128)}, f32[20,128,128]{2,1,0:T(8,128)S(1)}, u32[]{:S(2)}) copy-start(f32[20,128,128]{2,1,0:T(8,128)S(1)} %collective-permute-done.6.refs_4_) | copy-start | bytes 3932164
  62.8 21.6 %collective-permute-start.10 = (f32[20,128,128]{2,1,0:T(8,128)}, f32[20,128,128]{2,1,0:T(8,128)}, u32[]{:S(2)}, u32[]{:S(2)}) collective-permute-start(f32[20,128,128]{2,1,0:T(8,128)} %collective-permute-done.8.refs_7_), channel_id=1, source_target_pairs={{0,4},{4,0},{8,12},{12,8},{16,20},{20,16},{24,28},{28,24},{1,5},{5... | collective-permute-start | bytes 3932168 | tf_op jit(solution)/shard_map/ppermute | solution.py:224
  63.3 21.1 %collective-permute-start.9 = (f32[20,128,128]{2,1,0:T(8,128)S(1)}, f32[20,128,128]{2,1,0:T(8,128)}, u32[]{:S(2)}, u32[]{:S(2)}) collective-permute-start(f32[20,128,128]{2,1,0:T(8,128)S(1)} %collective-permute-done.7.refs_5_), channel_id=1, source_target_pairs={{0,4},{4,0},{8,12},{12,8},{16,20},{20,16},{24,28},{28,24},{1,5},{5... | collective-permute-start | bytes 3932168 | tf_op jit(solution)/shard_map/ppermute | solution.py:224
  65.4 37.0 %collective-permute-start.15 = (f32[12,128,128]{2,1,0:T(8,128)}, f32[12,128,128]{2,1,0:T(8,128)S(1)}, u32[]{:S(2)}, u32[]{:S(2)}) collective-permute-start(f32[12,128,128]{2,1,0:T(8,128)} %collective-permute-done.3), channel_id=1, source_target_pairs={{0,1},{1,0},{2,3},{3,2},{4,5},{5,4},{6,7},{7,6},{8,9},{9,8},{10,11... | collective-permute-start | bytes 2359304 | tf_op jit(solution)/shard_map/ppermute | solution.py:218
  79.3 2.7 %copy-start.7 = (f32[2,12,128,128]{3,2,1,0:T(8,128)}, f32[2,12,128,128]{3,2,1,0:T(8,128)S(1)}, u32[]{:S(2)}) copy-start(f32[2,12,128,128]{3,2,1,0:T(8,128)S(1)} %collective-permute-done.5.refs_2_) | copy-start | bytes 4718596
  79.3 34.0 %collective-permute-start.2 = (f32[12,128,128]{2,1,0:T(8,128)}, f32[12,128,128]{2,1,0:T(8,128)S(1)}, u32[]{:S(2)}, u32[]{:S(2)}) collective-permute-start(f32[12,128,128]{2,1,0:T(8,128)} %collective-permute-done.1), channel_id=1, source_target_pairs={{0,1},{1,0},{2,3},{3,2},{4,5},{5,4},{6,7},{7,6},{8,9},{9,8},{10,11... | collective-permute-start | bytes 2359304 | tf_op jit(solution)/shard_map/ppermute | solution.py:218
  81.1 0.9 copy-start.5
  82.0 2.4 %collective-permute-start.14 = (f32[10,128,128]{2,1,0:T(8,128)}, f32[10,128,128]{2,1,0:T(8,128)}, u32[]{:S(2)}, u32[]{:S(2)}) collective-permute-start(f32[10,128,128]{2,1,0:T(8,128)} %collective-permute-done.12.refs_10_), channel_id=1, source_target_pairs={{0,4},{4,0},{8,12},{12,8},{16,20},{20,16},{24,28},{28,24},{1,5},{5... | collective-permute-start | bytes 1966088 | tf_op jit(solution)/shard_map/ppermute | solution.py:224

commit v3 on v2

--- a/solution.py
+++ b/solution.py
@@ -151,7 +151,7 @@
 def add_panels(sizes, per_list, info, items, b_held, acc, ahead):
     _, a_slots, size, _ = items[0][0].shape
     steps = tuple((i, j, step, q + j) for i, (a, step, q) in enumerate(items) for j in range(a.shape[0]))
-    a_list = [in_hbm(a) for a, _, _ in items]
+    a_list = [in_hbm(a) if i != 1 else a for i, (a, _, _) in enumerate(items)]
     b_slots = sum(piece.shape[0] for piece in b_held[0])
     pieces, b_list = [], []
     for code, parts in enumerate(b_held):

time: 117 us -> 116 us (level)
  Pallas kernels: 23.5 us -> 25.1 us
  waiting for transfers between devices: 56.7 us -> 55.1 us
    ppermute x4, waiting for transfers between devices: 40 us -> 38.4 us  [over_even(): lax.ppermute(value, 'col', [(i, i ^ 1) for i in range(cols) if i ^ 1 < co...]
    pallas_call x2, Pallas kernels: 5.55 us -> 6.9 us  [add_ready(): pl.pallas_call(functools.partial(ready_kernel, sizes, per_list, step, q,...]
  transfers between devices with their start and end apart: 16 -> 16, of which waited for: 6 -> 5; matrix products, arithmetic and copies ran while one was open for 1% -> 2% of each run, Pallas kernels for 17% -> 18%
where the time goes in v3:
time: 116 us
  waiting for transfers between devices  55.1 us (48%)
  starting transfers between devices  32.1 us (28%)
  Pallas kernels  25.1 us (22%)
  local copies, waits for them, and re-layouts  3.34 us (3%)
    ppermute x4, waiting for transfers between devices, over_even(): lax.ppermute(value, 'col', [(i, i ^ 1) for i in range(cols) if i ^ 1 < co...  38.4 us
    ppermute x4, starting transfers between devices, over_even(): lax.ppermute(value, 'col', [(i, i ^ 1) for i in range(cols) if i ^ 1 < co...  22.2 us
    pallas_call x2, Pallas kernels, add_panels(): pl.pallas_call(functools.partial(panel_kernel, sizes, per_list, steps, tu...  18.2 us
    ppermute x9, waiting for transfers between devices, swap(): return lax.ppermute(value, 'row', [(i, i ^ bit) for i in range(rows)])  16.7 us
    pallas_call x2, Pallas kernels, add_ready(): pl.pallas_call(functools.partial(ready_kernel, sizes, per_list, step, q,...  6.9 us
    ppermute x9, starting transfers between devices, swap(): return lax.ppermute(value, 'row', [(i, i ^ bit) for i in range(rows)])  6.8 us
    ppermute x3, starting transfers between devices, over_odd(): lax.ppermute(value, 'col', [(i, j) for i in range(cols) for j in [(i + 1...  3.07 us
  transfers between devices with their start and end apart: 16, of which 5 were waited for; matrix products, arithmetic and copies ran while one was open for 2% of the time, Pallas kernels for 18%

profile of v3, /device:TPU:0, one launch (start us, length us, event | category | flops | bytes accessed | tf_op | source)
XLA Modules:
  0.0 116.1 jit_solution(18103569894883031995)
XLA Ops:
  0.0 3.0 %collective-permute-start = (f32[2,12,128,128]{3,2,1,0:T(8,128)}, f32[2,12,128,128]{3,2,1,0:T(8,128)S(1)}, u32[]{:S(2)}, u32[]{:S(2)}) collective-permute-start(f32[2,12,128,128]{3,2,1,0:T(8,128)} %bitcast.20), channel_id=1, source_target_pairs={{0,1},{1,0},{2,3},{3,2},{4,5},{5,4},{6,7},{7,6},{8,9},{9,8},{10,11... | collective-permute-start | bytes 4718600 | tf_op jit(solution)/shard_map/ppermute | solution.py:218
  3.0 0.7 collective-permute-start.4
  3.8 0.0 copy-start
  3.8 1.6 %collective-permute-start.7 = (f32[20,128,128]{2,1,0:T(8,128)}, f32[20,128,128]{2,1,0:T(8,128)}, u32[]{:S(2)}, u32[]{:S(2)}) collective-permute-start(f32[20,128,128]{2,1,0:T(8,128)} %bitcast.15), channel_id=1, source_target_pairs={{0,8},{4,12},{8,0},{12,4},{16,24},{20,28},{24,16},{28,20},{1,9},{5... | collective-permute-start | bytes 3932168 | tf_op jit(solution)/shard_map/ppermute | solution.py:224
  5.4 1.5 %collective-permute-start.8 = (f32[20,128,128]{2,1,0:T(8,128)}, f32[20,128,128]{2,1,0:T(8,128)}, u32[]{:S(2)}, u32[]{:S(2)}) collective-permute-start(f32[20,128,128]{2,1,0:T(8,128)} %bitcast.16), channel_id=1, source_target_pairs={{0,16},{4,20},{8,24},{12,28},{16,0},{20,4},{24,8},{28,12},{1,17},{... | collective-permute-start | bytes 3932168 | tf_op jit(solution)/shard_map/ppermute | solution.py:224
  6.9 30.8 %collective-permute-done.refs_1_ = f32[2,12,128,128]{3,2,1,0:T(8,128)S(1)} collective-permute-done((f32[2,12,128,128]{3,2,1,0:T(8,128)}, f32[2,12,128,128]{3,2,1,0:T(8,128)S(1)}, u32[]{:S(2)}, u32[]{:S(2)}) %collective-permute-start) | collective-permute-done | bytes 1572896 | tf_op jit(solution)/shard_map/ppermute | solution.py:218
  37.6 0.1 slice_bitcast_fusion
  37.8 0.0 copy-start.6
  37.8 1.6 %collective-permute-start.3 = (f32[12,128,128]{2,1,0:T(8,128)S(1)}, f32[12,128,128]{2,1,0:T(8,128)}, u32[]{:S(2)}, u32[]{:S(2)}) collective-permute-start(f32[12,128,128]{2,1,0:T(8,128)S(1)} %get-tuple-element.23), channel_id=1, source_target_pairs={{1,2},{2,1},{5,6},{6,5},{9,10},{10,9},{13,14},{14,13},{17,18},{18,... | collective-permute-start | bytes 2359304 | tf_op jit(solution)/shard_map/ppermute | solution.py:221
  39.4 0.0 copy-done
  39.4 0.0 collective-permute-start.6
  39.4 0.0 collective-permute-done.4.refs_2_
  39.4 0.0 copy-start.4
  39.4 3.8 %collective-permute-start.5 = (f32[2,12,128,128]{3,2,1,0:T(8,128)S(1)}, f32[2,12,128,128]{3,2,1,0:T(8,128)S(1)}, u32[]{:S(2)}, u32[]{:S(2)}) collective-permute-start(f32[2,12,128,128]{3,2,1,0:T(8,128)S(1)} %collective-permute-done.4.refs_2_), channel_id=1, source_target_pairs={{0,1},{1,0},{2,3},{3,2},{4,5},{5,4},{6,7},{7,6},{8,9},{9,8},{10,11... | collective-permute-start | bytes 4718600 | tf_op jit(solution)/shard_map/ppermute | solution.py:218
  43.2 0.0 collective-permute-done.7.refs_5_
  43.2 0.7 collective-permute-start.1
  43.9 0.0 collective-permute-done.8.refs_7_
  43.9 0.0 collective-permute-done.3
  43.9 1.1 slice.27
  45.1 1.6 %collective-permute-start.11 = (f32[10,128,128]{2,1,0:T(8,128)S(1)}, f32[10,128,128]{2,1,0:T(8,128)S(1)}, u32[]{:S(2)}, u32[]{:S(2)}) collective-permute-start(f32[10,128,128]{2,1,0:T(8,128)S(1)} %slice.27), channel_id=1, source_target_pairs={{0,16},{4,20},{8,24},{12,28},{16,0},{20,4},{24,8},{28,12},{1,17},{... | collective-permute-start | bytes 1966088 | tf_op jit(solution)/shard_map/ppermute | solution.py:224
  46.7 1.1 slice.28
  47.8 1.6 %collective-permute-start.12 = (f32[10,128,128]{2,1,0:T(8,128)S(1)}, f32[10,128,128]{2,1,0:T(8,128)}, u32[]{:S(2)}, u32[]{:S(2)}) collective-permute-start(f32[10,128,128]{2,1,0:T(8,128)S(1)} %slice.28), channel_id=1, source_target_pairs={{0,8},{4,12},{8,0},{12,4},{16,24},{20,28},{24,16},{28,20},{1,9},{5... | collective-permute-start | bytes 1966088 | tf_op jit(solution)/shard_map/ppermute | solution.py:224
  49.4 12.6 %collective-permute-done.11.refs_9_ = f32[10,128,128]{2,1,0:T(8,128)S(1)} collective-permute-done((f32[10,128,128]{2,1,0:T(8,128)S(1)}, f32[10,128,128]{2,1,0:T(8,128)S(1)}, u32[]{:S(2)}, u32[]{:S(2)}) %collective-permute-start.11) | collective-permute-done | bytes 655392 | tf_op jit(solution)/shard_map/ppermute | solution.py:224
  61.9 0.0 collective-permute-start.13
  61.9 0.0 collective-permute-done.6.refs_4_
  62.0 0.5 collective-permute-start.10
  62.4 0.0 collective-permute-done.1
  62.5 0.1 collective-permute-start.9
  62.5 1.9 %collective-permute-done.12.refs_10_ = f32[10,128,128]{2,1,0:T(8,128)} collective-permute-done((f32[10,128,128]{2,1,0:T(8,128)S(1)}, f32[10,128,128]{2,1,0:T(8,128)}, u32[]{:S(2)}, u32[]{:S(2)}) %collective-permute-start.12) | collective-permute-done | bytes 655392 | tf_op jit(solution)/shard_map/ppermute | solution.py:224
  64.5 14.1 %collective-permute-start.15 = (f32[12,128,128]{2,1,0:T(8,128)}, f32[12,128,128]{2,1,0:T(8,128)}, u32[]{:S(2)}, u32[]{:S(2)}) collective-permute-start(f32[12,128,128]{2,1,0:T(8,128)} %collective-permute-done.3), channel_id=1, source_target_pairs={{0,1},{1,0},{2,3},{3,2},{4,5},{5,4},{6,7},{7,6},{8,9},{9,8},{10,11... | collective-permute-start | bytes 2359304 | tf_op jit(solution)/shard_map/ppermute | solution.py:218
  78.6 0.0 collective-permute-done.5.refs_2_
  78.6 0.0 copy-start.5
  78.6 1.3 %collective-permute-start.2 = (f32[12,128,128]{2,1,0:T(8,128)S(1)}, f32[12,128,128]{2,1,0:T(8,128)S(1)}, u32[]{:S(2)}, u32[]{:S(2)}) collective-permute-start(f32[12,128,128]{2,1,0:T(8,128)S(1)} %collective-permute-done.1), channel_id=1, source_target_pairs={{0,1},{1,0},{2,3},{3,2},{4,5},{5,4},{6,7},{7,6},{8,9},{9,8},{10,11... | collective-permute-start | bytes 2359304 | tf_op jit(solution)/shard_map/ppermute | solution.py:218
  79.9 0.0 collective-permute-done.13.refs_11_
  79.9 0.8 copy-done.3
  80.8 0.0 collective-permute-start.14
  80.8 0.1 convert_reduce_fusion
  80.9 0.1 select_n.9
  81.0 0.1 pad_add_fusion.info
  81.1 2.1 %collective-permute-done.14.refs_12_ = f32[10,128,128]{2,1,0:T(8,128)} collective-permute-done((f32[10,128,128]{2,1,0:T(8,128)}, f32[10,128,128]{2,1,0:T(8,128)}, u32[]{:S(2)}, u32[]{:S(2)}) %collective-permute-start.14) | collective-permute-done | bytes 655392 | tf_op jit(solution)/shard_map/ppermute | solution.py:224
  83.2 0.0 collective-permute-done.10.refs_8_
  83.2 0.0 collective-permute-done.9.refs_6_
  83.2 10.2 %add_panels.2.refs_13_ = f32[49,128,128]{2,1,0:T(8,128)S(1)} custom-call(s32[522]{0:T(1024)S(1)} %pad_add_fusion.info, f32[2,12,128,128]{3,2,1,0:T(8,128)} %bitcast.22, f32[2,12,128,128]{3,2,1,0:T(8,128)S(1)} %collective-permute-done.refs_1_, f32[2,12,128,128]{3,2,1,0:T(8,128)} %copy-done.4, f32[20,128,128]{2,1,0:T(8,128)} %bitcast.17, ...), custom_call_target="tpu_custom_call" | custom-call | flops 65536 | bytes 65536 | tf_op jit(solution)/shard_map/add_panels/pallas_call | solution.py:166
  93.5 8.0 %add_panels.3 = (f32[49,128,128]{2,1,0:T(8,128)S(1)}, bf16[20,128,256]{2,1,0:T(8,128)(2,1)S(1)}, bf16[20,128,256]{2,1,0:T(8,128)(2,1)S(1)}) custom-call(s32[522]{0:T(1024)S(1)} %pad_add_fusion.info, f32[1,12,128,128]{3,2,1,0:T(8,128)} %bitcast.6.refs_0_, f32[1,12,128,128]{3,2,1,0:T(8,128)S(1)} %bitcast.14, ...), custom_call_target="tpu_custom_call", output_to_operand_aliasing={{0}: (14, {})} | custom-call | flops 65536 | bytes 65536 | tf_op jit(solution)/shard_map/add_panels/pallas_call | solution.py:166
  101.5 0.0 collective-permute-done.15.a_ref
  101.5 2.9 %add_last.2._ = f32[49,128,128]{2,1,0:T(8,128)S(1)} custom-call(s32[522]{0:T(1024)S(1)} %pad_add_fusion.info, f32[12,128,128]{2,1,0:T(8,128)} %collective-permute-done.15.a_ref, bf16[20,128,256]{2,1,0:T(8,128)(2,1)S(1)} %get-tuple-element.18.b_split, f32[49,128,128]{2,1,0:T(8,128)S(1)} %get-tuple-element.19._), custom_call_target="tpu_custom_call", output_to_operand_aliasing={{}: (3, {})} | custom-call | flops 65536 | bytes 65536 | tf_op jit(solution)/shard_map/add_last/pallas_call | solution.py:191
  104.4 7.7 %collective-permute-done.2.a_ref = f32[12,128,128]{2,1,0:T(8,128)S(1)} collective-permute-done((f32[12,128,128]{2,1,0:T(8,128)S(1)}, f32[12,128,128]{2,1,0:T(8,128)S(1)}, u32[]{:S(2)}, u32[]{:S(2)}) %collective-permute-start.2) | collective-permute-done | bytes 786464 | tf_op jit(solution)/shard_map/ppermute | solution.py:218
  112.1 4.0 %add_last.3 = (f32[49,128,128]{2,1,0:T(8,128)S(1)}, f32[48,128,128]{2,1,0:T(8,128)}) custom-call(s32[522]{0:T(1024)S(1)} %pad_add_fusion.info, f32[12,128,128]{2,1,0:T(8,128)S(1)} %collective-permute-done.2.a_ref, bf16[20,128,256]{2,1,0:T(8,128)(2,1)S(1)} %get-tuple-element.16.b_split, f32[49,128,128]{2,1,0:T(8,128)S(1)} %add_last.2._), custom_call_target="tpu_custom_call", output_to_operand_aliasing={{0}: (3, {})} | custom-call | flops 65536 | bytes 65536 | tf_op jit(solution)/shard_map/add_last/pallas_call | solution.py:191
  (9 shorter events, 0.0 us)
Async XLA Ops:
  0.0 37.6 %collective-permute-start = (f32[2,12,128,128]{3,2,1,0:T(8,128)}, f32[2,12,128,128]{3,2,1,0:T(8,128)S(1)}, u32[]{:S(2)}, u32[]{:S(2)}) collective-permute-start(f32[2,12,128,128]{3,2,1,0:T(8,128)} %bitcast.20), channel_id=1, source_target_pairs={{0,1},{1,0},{2,3},{3,2},{4,5},{5,4},{6,7},{7,6},{8,9},{9,8},{10,11... | collective-permute-start | bytes 4718600 | tf_op jit(solution)/shard_map/ppermute | solution.py:218
  3.0 36.4 %collective-permute-start.4 = (f32[2,12,128,128]{3,2,1,0:T(8,128)}, f32[2,12,128,128]{3,2,1,0:T(8,128)S(1)}, u32[]{:S(2)}, u32[]{:S(2)}) collective-permute-start(f32[2,12,128,128]{3,2,1,0:T(8,128)} %bitcast.21), channel_id=1, source_target_pairs={{1,2},{2,1},{5,6},{6,5},{9,10},{10,9},{13,14},{14,13},{17,18},{18,... | collective-permute-start | bytes 4718600 | tf_op jit(solution)/shard_map/ppermute | solution.py:221
  3.8 35.6 %copy-start = (f32[1,1,20,128,128]{4,3,2,1,0:T(8,128)S(1)}, f32[1,1,20,128,128]{4,3,2,1,0:T(8,128)}, u32[]{:S(2)}) copy-start(f32[1,1,20,128,128]{4,3,2,1,0:T(8,128)} %param.4) | copy-start | bytes 3932164
  3.8 39.4 %collective-permute-start.7 = (f32[20,128,128]{2,1,0:T(8,128)}, f32[20,128,128]{2,1,0:T(8,128)}, u32[]{:S(2)}, u32[]{:S(2)}) collective-permute-start(f32[20,128,128]{2,1,0:T(8,128)} %bitcast.15), channel_id=1, source_target_pairs={{0,8},{4,12},{8,0},{12,4},{16,24},{20,28},{24,16},{28,20},{1,9},{5... | collective-permute-start | bytes 3932168 | tf_op jit(solution)/shard_map/ppermute | solution.py:224
  5.4 38.6 %collective-permute-start.8 = (f32[20,128,128]{2,1,0:T(8,128)}, f32[20,128,128]{2,1,0:T(8,128)}, u32[]{:S(2)}, u32[]{:S(2)}) collective-permute-start(f32[20,128,128]{2,1,0:T(8,128)} %bitcast.16), channel_id=1, source_target_pairs={{0,16},{4,20},{8,24},{12,28},{16,0},{20,4},{24,8},{28,12},{1,17},{... | collective-permute-start | bytes 3932168 | tf_op jit(solution)/shard_map/ppermute | solution.py:224
  37.8 43.0 %copy-start.6 = (s32[1,1,8,64,3]{3,2,4,1,0:T(8,128)S(1)}, s32[1,1,8,64,3]{3,2,4,1,0:T(8,128)}, u32[]{:S(2)}) copy-start(s32[1,1,8,64,3]{3,2,4,1,0:T(8,128)} %param.5) | copy-start | bytes 18436
  37.8 6.1 %collective-permute-start.3 = (f32[12,128,128]{2,1,0:T(8,128)S(1)}, f32[12,128,128]{2,1,0:T(8,128)}, u32[]{:S(2)}, u32[]{:S(2)}) collective-permute-start(f32[12,128,128]{2,1,0:T(8,128)S(1)} %get-tuple-element.23), channel_id=1, source_target_pairs={{1,2},{2,1},{5,6},{6,5},{9,10},{10,9},{13,14},{14,13},{17,18},{18,... | collective-permute-start | bytes 2359304 | tf_op jit(solution)/shard_map/ppermute | solution.py:221
  39.4 22.5 %collective-permute-start.6 = (f32[20,128,128]{2,1,0:T(8,128)S(1)}, f32[20,128,128]{2,1,0:T(8,128)S(1)}, u32[]{:S(2)}, u32[]{:S(2)}) collective-permute-start(f32[20,128,128]{2,1,0:T(8,128)S(1)} %bitcast.19), channel_id=1, source_target_pairs={{0,4},{4,0},{8,12},{12,8},{16,20},{20,16},{24,28},{28,24},{1,5},{5... | collective-permute-start | bytes 3932168 | tf_op jit(solution)/shard_map/ppermute | solution.py:224
  39.4 41.4 %copy-start.4 = (f32[2,12,128,128]{3,2,1,0:T(8,128)}, f32[2,12,128,128]{3,2,1,0:T(8,128)S(1)}, u32[]{:S(2)}) copy-start(f32[2,12,128,128]{3,2,1,0:T(8,128)S(1)} %collective-permute-done.4.refs_2_) | copy-start | bytes 4718596
  39.4 39.2 %collective-permute-start.5 = (f32[2,12,128,128]{3,2,1,0:T(8,128)S(1)}, f32[2,12,128,128]{3,2,1,0:T(8,128)S(1)}, u32[]{:S(2)}, u32[]{:S(2)}) collective-permute-start(f32[2,12,128,128]{3,2,1,0:T(8,128)S(1)} %collective-permute-done.4.refs_2_), channel_id=1, source_target_pairs={{0,1},{1,0},{2,3},{3,2},{4,5},{5,4},{6,7},{7,6},{8,9},{9,8},{10,11... | collective-permute-start | bytes 4718600 | tf_op jit(solution)/shard_map/ppermute | solution.py:218
  43.2 19.2 %collective-permute-start.1 = (f32[12,128,128]{2,1,0:T(8,128)S(1)}, f32[12,128,128]{2,1,0:T(8,128)S(1)}, u32[]{:S(2)}, u32[]{:S(2)}) collective-permute-start(f32[12,128,128]{2,1,0:T(8,128)S(1)} %get-tuple-element.24), channel_id=1, source_target_pairs={{1,2},{2,1},{5,6},{6,5},{9,10},{10,9},{13,14},{14,13},{17,18},{18,... | collective-permute-start | bytes 2359304 | tf_op jit(solution)/shard_map/ppermute | solution.py:221
  45.1 16.9 %collective-permute-start.11 = (f32[10,128,128]{2,1,0:T(8,128)S(1)}, f32[10,128,128]{2,1,0:T(8,128)S(1)}, u32[]{:S(2)}, u32[]{:S(2)}) collective-permute-start(f32[10,128,128]{2,1,0:T(8,128)S(1)} %slice.27), channel_id=1, source_target_pairs={{0,16},{4,20},{8,24},{12,28},{16,0},{20,4},{24,8},{28,12},{1,17},{... | collective-permute-start | bytes 1966088 | tf_op jit(solution)/shard_map/ppermute | solution.py:224
  47.8 16.7 %collective-permute-start.12 = (f32[10,128,128]{2,1,0:T(8,128)S(1)}, f32[10,128,128]{2,1,0:T(8,128)}, u32[]{:S(2)}, u32[]{:S(2)}) collective-permute-start(f32[10,128,128]{2,1,0:T(8,128)S(1)} %slice.28), channel_id=1, source_target_pairs={{0,8},{4,12},{8,0},{12,4},{16,24},{20,28},{24,16},{28,20},{1,9},{5... | collective-permute-start | bytes 1966088 | tf_op jit(solution)/shard_map/ppermute | solution.py:224
  61.9 16.7 %copy-start.2 = (f32[10,128,128]{2,1,0:T(8,128)}, f32[10,128,128]{2,1,0:T(8,128)S(1)}, u32[]{:S(2)}) copy-start(f32[10,128,128]{2,1,0:T(8,128)S(1)} %collective-permute-done.11.refs_9_) | copy-start | bytes 1966084
  61.9 18.0 %collective-permute-start.13 = (f32[10,128,128]{2,1,0:T(8,128)S(1)}, f32[10,128,128]{2,1,0:T(8,128)S(1)}, u32[]{:S(2)}, u32[]{:S(2)}) collective-permute-start(f32[10,128,128]{2,1,0:T(8,128)S(1)} %collective-permute-done.11.refs_9_), channel_id=1, source_target_pairs={{0,4},{4,0},{8,12},{12,8},{16,20},{20,16},{24,28},{28,24},{1,5},{5... | collective-permute-start | bytes 1966088 | tf_op jit(solution)/shard_map/ppermute | solution.py:224
  61.9 16.6 %copy-start.1 = (f32[20,128,128]{2,1,0:T(8,128)}, f32[20,128,128]{2,1,0:T(8,128)S(1)}, u32[]{:S(2)}) copy-start(f32[20,128,128]{2,1,0:T(8,128)S(1)} %collective-permute-done.6.refs_4_) | copy-start | bytes 3932164
  62.0 21.3 %collective-permute-start.10 = (f32[20,128,128]{2,1,0:T(8,128)}, f32[20,128,128]{2,1,0:T(8,128)}, u32[]{:S(2)}, u32[]{:S(2)}) collective-permute-start(f32[20,128,128]{2,1,0:T(8,128)} %collective-permute-done.8.refs_7_), channel_id=1, source_target_pairs={{0,4},{4,0},{8,12},{12,8},{16,20},{20,16},{24,28},{28,24},{1,5},{5... | collective-permute-start | bytes 3932168 | tf_op jit(solution)/shard_map/ppermute | solution.py:224
  62.5 20.8 %collective-permute-start.9 = (f32[20,128,128]{2,1,0:T(8,128)}, f32[20,128,128]{2,1,0:T(8,128)}, u32[]{:S(2)}, u32[]{:S(2)}) collective-permute-start(f32[20,128,128]{2,1,0:T(8,128)} %collective-permute-done.7.refs_5_), channel_id=1, source_target_pairs={{0,4},{4,0},{8,12},{12,8},{16,20},{20,16},{24,28},{28,24},{1,5},{5... | collective-permute-start | bytes 3932168 | tf_op jit(solution)/shard_map/ppermute | solution.py:224
  64.5 37.0 %collective-permute-start.15 = (f32[12,128,128]{2,1,0:T(8,128)}, f32[12,128,128]{2,1,0:T(8,128)}, u32[]{:S(2)}, u32[]{:S(2)}) collective-permute-start(f32[12,128,128]{2,1,0:T(8,128)} %collective-permute-done.3), channel_id=1, source_target_pairs={{0,1},{1,0},{2,3},{3,2},{4,5},{5,4},{6,7},{7,6},{8,9},{9,8},{10,11... | collective-permute-start | bytes 2359304 | tf_op jit(solution)/shard_map/ppermute | solution.py:218
  78.6 2.2 %copy-start.5 = (f32[2,12,128,128]{3,2,1,0:T(8,128)}, f32[2,12,128,128]{3,2,1,0:T(8,128)S(1)}, u32[]{:S(2)}) copy-start(f32[2,12,128,128]{3,2,1,0:T(8,128)S(1)} %collective-permute-done.5.refs_2_) | copy-start | bytes 4718596
  78.6 33.5 %collective-permute-start.2 = (f32[12,128,128]{2,1,0:T(8,128)S(1)}, f32[12,128,128]{2,1,0:T(8,128)S(1)}, u32[]{:S(2)}, u32[]{:S(2)}) collective-permute-start(f32[12,128,128]{2,1,0:T(8,128)S(1)} %collective-permute-done.1), channel_id=1, source_target_pairs={{0,1},{1,0},{2,3},{3,2},{4,5},{5,4},{6,7},{7,6},{8,9},{9,8},{10,11... | collective-permute-start | bytes 2359304 | tf_op jit(solution)/shard_map/ppermute | solution.py:218
  79.9 0.8 copy-start.3
  80.8 2.4 %collective-permute-start.14 = (f32[10,128,128]{2,1,0:T(8,128)}, f32[10,128,128]{2,1,0:T(8,128)}, u32[]{:S(2)}, u32[]{:S(2)}) collective-permute-start(f32[10,128,128]{2,1,0:T(8,128)} %collective-permute-done.12.refs_10_), channel_id=1, source_target_pairs={{0,4},{4,0},{8,12},{12,8},{16,20},{20,16},{24,28},{28,24},{1,5},{5... | collective-permute-start | bytes 1966088 | tf_op jit(solution)/shard_map/ppermute | solution.py:224
